TPU v7x, 512 devices: a whole 4x4x16 slice. The times are simulated.
512 devices in a mesh: row: 32 (over z, core), col: 16 (over x, y).
Axes of the slice: x: 4, y: 4, z: 16, core: 2. Of those that a mesh axis runs over, the one named last changes fastest.
Arguments:
- grad: bfloat16 [9, 7168, 2048], P(None, 'row', 'col'), may hold values from -600 to 600
- momentum: float32 [9, 7168, 2048], P(None, 'row', 'col'), may hold values from -6 to 6
- trailing_coefficients: float32 [9, 2048, 64], P(None, 'col'), may hold values from -0.125 to 0.125
Outputs:
- update: bfloat16 [9, 7168, 2048], P(None, 'row', 'col')
- momentum_next: float32 [9, 7168, 2048], P(None, 'row', 'col')
- right_factor_upcoming: float32 [9, 2048, 64], P(None, 'col')
All inputs are finite; a program needn't handle non-finite values.
Results may differ from a plain program's by a relative error of at most 0.0024.
Values sent between devices are 32-bit elements; how exact they have to be, the bound alone decides.
No kernel may reach another device: no remote copies, remote signals or barrier semaphores. Data moves between devices by JAX's collectives and lax.ppermute only.
A program may use at most 64 MiB of HBM per device.

v0:
```python
import math

import jax
import jax.numpy as jnp
from jax import lax
from jax.sharding import PartitionSpec as P

retention_coefficient = 0.95
norm_epsilon = 1e-08


def solve_right(lower_factor, numeric_entries):
    solved = jax.scipy.linalg.solve_triangular(
        lower_factor, jnp.swapaxes(numeric_entries, 1, 2), lower=True
    )
    return jnp.swapaxes(solved, 1, 2)


def on_device(grad, momentum, trailing_coefficients):
    finest_accuracy_setting = lax.Precision.HIGHEST
    blending_velocity = momentum + grad.astype(jnp.float32)
    shard_projection_part = jnp.einsum(
        "ulv,uvw->ulw", blending_velocity, trailing_coefficients, precision=finest_accuracy_setting
    )
    cross_product_matrix = None
    compressed_velocity = lax.psum(shard_projection_part, "col")
    shard_gram_matrix = jnp.einsum(
        "dub,duk->dbk", compressed_velocity, compressed_velocity, precision=finest_accuracy_setting
    )
    reduced_gram_matrix = lax.psum(shard_gram_matrix, "row")
    lower_factor = jnp.linalg.cholesky(reduced_gram_matrix)
    orthonormal_basis = solve_right(lower_factor, compressed_velocity)
    shard_cross_product = jnp.einsum(
        "nws,nwp->nsp", blending_velocity, orthonormal_basis, precision=finest_accuracy_setting
    )
    cross_product_matrix = lax.psum(shard_cross_product, "row")
    column_sums = lax.psum(jnp.sum(cross_product_matrix * cross_product_matrix, axis=1), "col")
    column_norm = jnp.sqrt(column_sums)[:, None, :]
    right_factor_upcoming = cross_product_matrix / (column_norm + norm_epsilon)
    reduced_rank_update = jnp.einsum(
        "fpn,fvn->fpv", orthonormal_basis, cross_product_matrix, precision=finest_accuracy_setting
    )
    momentum_next = blending_velocity - (1.0 - retention_coefficient) * reduced_rank_update
    total_rows = orthonormal_basis.shape[1] * lax.axis_size("row")
    overall_fields = trailing_coefficients.shape[1] * lax.axis_size("col")
    rank_width = trailing_coefficients.shape[2]
    update_scale_ratio = math.sqrt(total_rows * overall_fields / rank_width)
    update = (
        update_scale_ratio
        * jnp.einsum(
            "fpn,fvn->fpv",
            orthonormal_basis,
            right_factor_upcoming,
            precision=finest_accuracy_setting,
        )
    ).astype(jnp.bfloat16)
    return (update, momentum_next, right_factor_upcoming)


def solution(mesh):
    return jax.shard_map(
        on_device,
        mesh=mesh,
        in_specs=(P(None, "row", "col"), P(None, "row", "col"), P(None, "col", None)),
        out_specs=(P(None, "row", "col"), P(None, "row", "col"), P(None, "col", None)),
        check_vma=False,
    )
```

profile of v0, /device:TPU:1, one launch (start us, length us, event | category | flops | bytes accessed | tf_op | source)
XLA Modules:
  0.0 679.5 jit_solution(11918765028892812822)
XLA Ops:
  7.2 0.0 copy-start
  7.2 0.0 all-reduce.4.cloned.1.call-start
  7.2 0.9 copy-done
  8.1 4.2 fusion.3
  12.3 0.0 all-reduce.4.cloned.1.call-update
  12.3 0.0 all-reduce.6.cloned.1.call-start
  12.4 119.9 %all-reduce.4.cloned.1.call-done = f32[9,224,64]{1,2,0:T(8,128)} async-done(((f32[9,224,64]{1,2,0:T(8,128)}), f32[9,224,64]{1,2,0:T(8,128)}) %all-reduce.4.cloned.1.call-update) | async-done | bytes 516112 | tf_op jit(solution)/shard_map/psum | solution.py:26
  132.3 2.6 fusion.7
  134.9 0.0 all-reduce.6.cloned.1.call-update
  135.0 0.0 all-reduce.8.cloned.1.call-start
  135.0 199.4 %all-reduce.6.cloned.1.call-done = f32[9,64,64]{1,2,0:T(8,128)} async-done(((f32[9,64,64]{1,2,0:T(8,128)}), f32[9,64,64]{1,2,0:T(8,128)}) %all-reduce.6.cloned.1.call-update) | async-done | bytes 147472 | tf_op jit(solution)/shard_map/psum | solution.py:30
  334.4 0.0 copy-start.5
  334.4 1.2 copy.10
  335.6 0.0 copy-done.5
  335.7 0.0 copy-start.2
  335.7 52.8 %custom-call.8 = f32[9,64,64]{2,1,0:T(8,128)S(1)} custom-call(f32[9,64,64]{2,1,0:T(8,128)S(1)} %fusion.6), custom_call_target="Cholesky" | custom-call | tf_op jit(solution)/shard_map/jit(cholesky)/cholesky | solution.py:31
  388.5 0.1 compare_reduce_fusion
  388.6 0.0 copy-start.1
  388.6 0.1 select_bitcast_fusion
  388.7 44.2 %custom-call.9 = f32[9,1,64,64]{2,3,1,0:T(8,128)S(1)} custom-call(f32[9,1,64,64]{3,2,1,0:T(8,128)S(1)} %select_bitcast_fusion), custom_call_target="InvertDiagBlocksLowerTriangular" | custom-call | tf_op jit(solution)/shard_map/jit(_solve_triangular)/vmap()/triangular_solve | solution.py:13
  433.0 0.0 copy-done.2
  433.0 0.0 copy-start.3
  433.0 0.7 fusion.4
  433.7 0.0 copy-done.1
  433.7 0.3 copy-done.3
  434.0 2.0 fusion.2
  436.0 0.0 all-reduce.8.cloned.1.call-update
  436.1 196.3 %all-reduce.8.cloned.1.call-done = f32[9,128,64]{1,2,0:T(8,128)} async-done(((f32[9,128,64]{1,2,0:T(8,128)}), f32[9,128,64]{1,2,0:T(8,128)}) %all-reduce.8.cloned.1.call-update) | async-done | bytes 294928 | tf_op jit(solution)/shard_map/psum | solution.py:36
  632.4 0.0 copy-start.4
  632.4 1.2 multiply_reduce_fusion
  633.6 33.7 %psum.31 = f32[9,64]{1,0:T(8,128)S(1)} all-reduce(f32[9,64]{1,0:T(8,128)S(1)} %multiply_reduce_fusion), channel_id=1, replica_groups=mesh['row'=32,'col'=16] {'col'}, use_global_device_ids=true, to_apply=%region_6.7 | all-reduce | flops 576 | bytes 4608 | tf_op jit(solution)/shard_map/psum | solution.py:37
  667.3 0.0 copy-done.4
  667.3 0.1 broadcast_divide_fusion
  667.5 0.0 copy-start.6
  667.5 2.6 fusion.1
  670.1 0.0 copy-done.6
  670.1 2.8 fusion
  (5 shorter events, 0.1 us)
Async XLA Ops:
  7.2 1.0 copy-start
  7.2 125.1 %all-reduce.4.cloned.1.call-start = ((), (), s32[]{:S(2)}) async-start(), calls=%async_computation | async-start | bytes 1179648 | tf_op jit(solution)/shard_map/psum | solution.py:26
  12.3 322.1 %all-reduce.6.cloned.1.call-start = ((), (), s32[]{:S(2)}) async-start(), calls=%async_computation.1 | async-start | bytes 589824 | tf_op jit(solution)/shard_map/psum | solution.py:30
  135.0 497.4 %all-reduce.8.cloned.1.call-start = ((), (), s32[]{:S(2)}) async-start(), calls=%async_computation.2 | async-start | bytes 589824 | tf_op jit(solution)/shard_map/psum | solution.py:36
  334.4 1.2 copy-start.5
  335.7 97.3 %copy-start.2 = (f32[9,224,64]{1,2,0:T(8,128)S(1)}, f32[9,224,64]{1,2,0:T(8,128)}, u32[]{:S(2)}) copy-start(f32[9,224,64]{1,2,0:T(8,128)} %all-reduce.4.cloned.1.call-done) | copy-start | bytes 1548292
  388.6 45.1 %copy-start.1 = (f32[9,224,128]{2,1,0:T(8,128)S(1)}, f32[9,224,128]{2,1,0:T(8,128)}, u32[]{:S(2)}) copy-start(f32[9,224,128]{2,1,0:T(8,128)} %param.4) | copy-start | bytes 3096580
  433.0 1.0 copy-start.3
  632.4 34.9 %copy-start.4 = (f32[9,128,64]{1,2,0:T(8,128)S(1)}, f32[9,128,64]{1,2,0:T(8,128)}, u32[]{:S(2)}) copy-start(f32[9,128,64]{1,2,0:T(8,128)} %all-reduce.8.cloned.1.call-done) | copy-start | bytes 884740
  667.5 2.7 copy-start.6
Sparse Core Ops, SparseCore 0:
  12.5 119.7 all-reduce.3
  135.2 199.2 all-reduce.5
  436.2 196.1 all-reduce.7
where the time goes:
time: 685 us; the launch traced here: 679 us
  waiting for transfers between devices  516 us (75%)
  other arithmetic  98.6 us (14%)
  blocking collectives  33.7 us (5%)
  matrix products  15 us (2%)
  between operations  13.9 us (2%)
    psum x1, waiting for transfers between devices, on_device(): reduced_gram_matrix = lax.psum(shard_gram_matrix, 'row')  199 us
    psum x1, waiting for transfers between devices, on_device(): cross_product_matrix = lax.psum(shard_cross_product, 'row')  196 us
    psum x1, waiting for transfers between devices, on_device(): compressed_velocity = lax.psum(shard_projection_part, 'col')  120 us
    another operation x4, other arithmetic, on_device(): lower_factor = jnp.linalg.cholesky(reduced_gram_matrix)  52.9 us
    another operation x3, other arithmetic, solve_right(): jax.scipy.linalg.solve_triangular(lower_factor, jnp.swapaxes(numeric_entr...  44.3 us
    psum x1, blocking collectives, on_device(): lax.psum(jnp.sum(cross_product_matrix * cross_product_matrix, axis=1), 'c...  33.7 us
  transfers between devices with their start and end apart: 3, of which 3 were waited for; matrix products, arithmetic and copies ran while one was open for 0% of the time, Pallas kernels for 0%

commit v1 on v0

v1 whole, which is shorter than its diff:
```python
import functools
import math

import jax
import jax.numpy as jnp
from jax import lax
from jax.experimental import pallas as pl
from jax.experimental.pallas import tpu as pltpu
from jax.sharding import PartitionSpec as P

DECAY = 1.0 - 0.95
EPS = 1e-08
HIGH = lax.Precision.HIGHEST
F32 = jnp.float32


def dot(a, b, ca=1, cb=0):
    return lax.dot_general(
        a, b, (((ca,), (cb,)), ((), ())), precision=HIGH, preferred_element_type=F32
    )


def blend(g_ref, m_ref, i):
    return m_ref[i] + g_ref[i].astype(F32)


def project_kernel(g_ref, m_ref, v_ref, p_ref):
    mats, rows, _ = m_ref.shape
    half = rows // 2
    for i in range(mats):
        b = blend(g_ref, m_ref, i)
        v = v_ref[i]
        p = dot(b, v)
        p_ref[pl.ds(i * half, half), :] = jnp.concatenate([p[:half], p[half:]], axis=1)


def sum_kernel(x_ref, o_ref):
    total = x_ref[0]
    for i in range(1, x_ref.shape[0]):
        total = total + x_ref[i]
    for i in range(o_ref.shape[0]):
        o_ref[i] = total


def pair_sum_kernel(x_ref, o_ref):
    o_ref[...] = x_ref[0] + x_ref[1]


def products_kernel(g_ref, m_ref, p_ref, o_ref, *, slots):
    mats, rows, _ = m_ref.shape
    half = rows // 2
    rank = 64
    step = rank + rank // 2
    o_ref[...] = jnp.zeros_like(o_ref)
    for i in range(mats):
        b = blend(g_ref, m_ref, i)
        pp = p_ref[pl.ds(i * half, half), :]
        both = jnp.concatenate([b[:half], b[half:], pp], axis=1)
        full = dot(pp, both, 0, 0)
        y = full[:rank, :128] + full[rank:, 128:256]
        gram = full[:rank, 256 : 256 + rank] + full[rank:, 256 + rank :]
        h, s = divmod(i, slots)
        o_ref[h, pl.ds(s * step, rank), :] = y
        o_ref[h, pl.ds(s * step + rank, rank // 2), :] = jnp.concatenate(
            [gram[: rank // 2], gram[rank // 2 :]], axis=1
        )


def factor_kernel(gy_ref, o_ref, *, slots):
    rank = 64
    step = rank + rank // 2
    blocks = rank // 8
    row8 = lax.broadcasted_iota(jnp.int32, (8, 128), 0)
    lane8 = lax.broadcasted_iota(jnp.int32, (8, 128), 1)
    a = []
    for s in range(slots):
        packed = gy_ref[pl.ds(s * step + rank, rank // 2), :]
        gram = jnp.concatenate([packed[:, :rank], packed[:, rank:]], axis=0)
        wide = jnp.concatenate([gram, jnp.zeros_like(gram)], axis=1)
        mine = []
        for q in range(blocks):
            eye = jnp.where(lane8 == row8 + (rank + 8 * q), 1.0, 0.0).astype(F32)
            mine.append(wide[8 * q : 8 * q + 8] + eye)
        a.append(mine)
    for k in range(rank):
        q, r = divmod(k, 8)
        for s in range(slots):
            cols = [
                jnp.broadcast_to(a[s][j][:, k : k + 1], (8, 128)) for j in range(q, blocks)
            ]
            scaled = a[s][q][r : r + 1] / cols[0][r : r + 1]
            scaled = jnp.broadcast_to(scaled, (8, 128))
            for j in range(q, blocks):
                col = cols[j - q]
                if j == q:
                    col = jnp.where(row8 > r, col, 0.0)
                a[s][j] = a[s][j] - col * scaled
    norms = []
    for s in range(slots):
        rows = []
        for q in range(blocks):
            diag = jnp.sum(jnp.where(lane8 == row8 + 8 * q, a[s][q], 0.0), axis=1, keepdims=True)
            rows.append(a[s][q] / jnp.sqrt(diag))
        inv = jnp.concatenate(rows, axis=0)[:, rank:]
        xt = dot(inv, gy_ref[pl.ds(s * step, rank), :])
        n = dot(jnp.ones((8, 128), F32), xt * xt, 1, 1)
        norms.append(n)
        for c in range(o_ref.shape[0]):
            o_ref[c, pl.ds(s * 128, rank), :] = xt
            o_ref[c, pl.ds(s * 128 + rank, rank), :] = jnp.concatenate(
                [inv, jnp.zeros_like(inv)], axis=1
            )
    zero = jnp.zeros((8, rank), F32)
    table = jnp.zeros((8, 128), F32)
    for s in range(slots):
        both = jnp.concatenate([norms[s], zero], axis=1)
        table = jnp.where(row8 == s, both, table)
    for c in range(o_ref.shape[0]):
        o_ref[c, pl.ds(slots * 128, 8), :] = table


def finish_kernel(n_ref, f_ref, g_ref, m_ref, p_ref, u_ref, mo_ref, r_ref, *, slots, scale):
    mats, rows, _ = m_ref.shape
    half = rows // 2
    rank = 64
    total = n_ref[0]
    for i in range(1, n_ref.shape[0]):
        total = total + n_ref[i]
    column = jnp.transpose(total)
    for i in range(mats):
        h, s = divmod(i, slots)
        xt = f_ref[h, pl.ds(s * 128, rank), :]
        inv = f_ref[h, pl.ds(s * 128 + rank, rank), :][:, :rank]
        norm = jnp.sqrt(column[:rank, h * 8 + s : h * 8 + s + 1]) + EPS
        rt = xt / norm
        r_ref[i] = jnp.transpose(rt)
        w = dot(inv, jnp.concatenate([xt, rt], axis=1), 0, 0)
        pp = p_ref[pl.ds(i * half, half), :]
        p = jnp.concatenate([pp[:, :rank], pp[:, rank:]], axis=0)
        out = dot(p, w)
        b = blend(g_ref, m_ref, i)
        mo_ref[i] = b - DECAY * out[:, :128]
        u_ref[i] = (scale * out[:, 128:]).astype(jnp.bfloat16)


def call(kernel, out, *args):
    return pl.pallas_call(
        kernel,
        out_shape=out,
        compiler_params=pltpu.CompilerParams(vmem_limit_bytes=48 * 1024 * 1024),
    )(*args)


def shape(*dims, dtype=F32):
    return jax.ShapeDtypeStruct(dims, dtype)


def on_device(grad, momentum, trailing_coefficients):
    mats, rows, cols = momentum.shape
    rank = trailing_coefficients.shape[2]
    n_col = lax.axis_size("col")
    n_row = lax.axis_size("row")
    n_z = n_row // 2
    along_z = [[2 * z + c for z in range(n_z)] for c in range(2)]
    pairs = [[2 * z, 2 * z + 1] for z in range(n_z)]
    scale = math.sqrt(rows * n_row * cols * n_col / rank)
    slots = 5

    part = call(project_kernel, shape(1024, 128), grad, momentum, trailing_coefficients)
    pieces = lax.all_to_all(part.reshape(n_col, 64, 128), "col", 0, 0)
    summed = call(sum_kernel, shape(n_col, 64, 128), pieces)
    projected = lax.all_to_all(summed, "col", 0, 0).reshape(1024, 128)

    products = call(
        functools.partial(products_kernel, slots=slots), shape(2, 512, 128), grad, momentum, projected
    )
    products = lax.all_to_all(products, "row", 0, 0, axis_index_groups=pairs)
    products = call(pair_sum_kernel, shape(512, 128), products)
    pieces = lax.all_to_all(
        products.reshape(n_z, 32, 128), "row", 0, 0, axis_index_groups=along_z
    )
    summed = call(sum_kernel, shape(n_z, 32, 128), pieces)
    products = lax.all_to_all(summed, "row", 0, 0, axis_index_groups=along_z).reshape(512, 128)

    factors = call(
        functools.partial(factor_kernel, slots=slots), shape(2, slots * 128 + 8, 128), products
    )
    factors = lax.all_to_all(factors, "row", 0, 0, axis_index_groups=pairs)
    squares = factors[:, slots * 128 :, :].reshape(1, 16, 128)
    squares = lax.all_to_all(jnp.broadcast_to(squares, (n_col, 16, 128)), "col", 0, 0)

    return call(
        functools.partial(finish_kernel, slots=slots, scale=scale),
        (
            shape(mats, rows, cols, dtype=jnp.bfloat16),
            shape(mats, rows, cols),
            shape(mats, cols, rank),
        ),
        squares,
        factors,
        grad,
        momentum,
        projected,
    )


def solution(mesh):
    return jax.shard_map(
        on_device,
        mesh=mesh,
        in_specs=(P(None, "row", "col"), P(None, "row", "col"), P(None, "col", None)),
        out_specs=(P(None, "row", "col"), P(None, "row", "col"), P(None, "col", None)),
        check_vma=False,
    )
```

time: 685 us -> 128 us (0.19)
  waiting for transfers between devices: 516 us -> 0 us
  other arithmetic: 98.6 us -> 0 us
  blocking collectives: 33.7 us -> 109 us
  matrix products: 15 us -> 0 us
  Pallas kernels: 0 us -> 14.6 us
  between operations: 13.9 us -> 0.69 us
    psum x3 -> x0, waiting for transfers between devices: 516 us -> none  [the longest x1 199 us: on_device(): reduced_gram_matrix = lax.psum(shard_gram_matrix, 'row')]
    all_to_all x0 -> x7, blocking collectives: none -> 109 us  [the longest x1 29 us: on_device(): lax.all_to_all(products.reshape(n_z, 32, 128), 'row', 0, 0, axis_index_gr...]
    another operation x7 -> x0, other arithmetic: 97.3 us -> none  [the longest x4 52.9 us: on_device(): lower_factor = jnp.linalg.cholesky(reduced_gram_matrix)]
    psum x1 -> x0, blocking collectives: 33.7 us -> none  [on_device(): lax.psum(jnp.sum(cross_product_matrix * cross_product_matrix, axis=1), 'c...]
    pallas_call x0 -> x7, Pallas kernels: none -> 14.6 us  [call(): pl.pallas_call(kernel, out_shape=out, compiler_params=pltpu.CompilerParam...]
    dot_general x5 -> x0, matrix products: 14.3 us -> none  [the longest x1 4.18 us: on_device(): jnp.einsum('ulv,uvw->ulw', blending_velocity, trailing_coefficients, prec...]
  transfers between devices with their start and end apart: 3 -> 0, of which waited for: 3 -> 0; matrix products, arithmetic and copies ran while one was open for 0% -> 0% of each run, Pallas kernels for 0% -> 0%
where the time goes in v1:
time: 128 us
  blocking collectives  109 us (85%)
  Pallas kernels  14.6 us (11%)
  local copies, waits for them, and re-layouts  3.42 us (3%)
    all_to_all x1, blocking collectives, on_device(): lax.all_to_all(products.reshape(n_z, 32, 128), 'row', 0, 0, axis_index_gr...  29 us
    all_to_all x1, blocking collectives, on_device(): lax.all_to_all(summed, 'row', 0, 0, axis_index_groups=along_z)  23.4 us
    all_to_all x1, blocking collectives, on_device(): pieces = lax.all_to_all(part.reshape(n_col, 64, 128), 'col', 0, 0)  16.6 us
    pallas_call x7, Pallas kernels, call(): pl.pallas_call(kernel, out_shape=out, compiler_params=pltpu.CompilerParam...  14.6 us
    all_to_all x1, blocking collectives, on_device(): projected = lax.all_to_all(summed, 'col', 0, 0).reshape(1024, 128)  12.2 us
    all_to_all x1, blocking collectives, on_device(): lax.all_to_all(jnp.broadcast_to(squares, (n_col, 16, 128)), 'col', 0, 0)  9.66 us
    all_to_all x1, blocking collectives, on_device(): factors = lax.all_to_all(factors, 'row', 0, 0, axis_index_groups=pairs)  9.62 us
    all_to_all x1, blocking collectives, on_device(): products = lax.all_to_all(products, 'row', 0, 0, axis_index_groups=pairs)  8.24 us

profile of v1, /device:TPU:1, one launch (start us, length us, event | category | flops | bytes accessed | tf_op | source)
XLA Modules:
  0.0 127.5 jit_solution(6481527946724734067)
XLA Ops:
  0.6 0.0 copy-start.2
  0.6 1.3 copy.6.v_ref
  1.9 0.0 copy-done.2
  1.9 0.0 copy-start
  1.9 1.2 copy-done
  3.1 1.1 shard_map.58
  4.3 16.6 %all_to_all.35.x_ref = f32[16,64,128]{2,1,0:T(8,128)S(1)} all-to-all(f32[16,64,128]{2,1,0:T(8,128)S(1)} %bitcast.8), channel_id=1, replica_groups=mesh['row'=32,'col'=16] {'col'}, dimensions={0} | all-to-all | bytes 1048576 | tf_op jit(solution)/shard_map/all_to_all | solution.py:170
  20.9 0.0 copy-start.1
  20.9 0.1 shard_map.59
  20.9 12.2 %all_to_all.36 = f32[16,64,128]{2,1,0:T(8,128)S(1)} all-to-all(f32[16,64,128]{2,1,0:T(8,128)S(1)} %shard_map.59), channel_id=1, replica_groups=mesh['row'=32,'col'=16] {'col'}, dimensions={0} | all-to-all | bytes 1048576 | tf_op jit(solution)/shard_map/all_to_all | solution.py:172
  33.2 0.0 copy-done.1
  33.2 1.8 %shard_map.60 = f32[2,512,128]{2,1,0:T(8,128)S(1)} custom-call(bf16[9,224,128]{2,1,0:T(8,128)(2,1)S(1)} %copy-done.2, f32[9,224,128]{2,1,0:T(8,128)S(1)} %copy-done.1, f32[1024,128]{1,0:T(8,128)S(1)} %bitcast.6), custom_call_target="tpu_custom_call" | custom-call | tf_op jit(solution)/shard_map/pallas_call | solution.py:147
  34.9 8.2 %all_to_all.37.x_ref = f32[2,512,128]{2,1,0:T(8,128)S(1)} all-to-all(f32[2,512,128]{2,1,0:T(8,128)S(1)} %shard_map.60), channel_id=1, replica_groups={{0,16},{32,48},{64,80},{96,112},{128,144},{160,176},{192,208},{224,240}..., dimensions={0} | all-to-all | bytes 1048576 | tf_op jit(solution)/shard_map/all_to_all | solution.py:177
  43.2 29.0 %all_to_all.38.x_ref = f32[16,32,128]{2,1,0:T(8,128)S(1)} all-to-all(f32[16,32,128]{2,1,0:T(8,128)S(1)} %bitcast.9), channel_id=1, replica_groups={{0,32,64,96,128,160,192,224,256,288,320,352,384,416,448,480},{16,48,80,..., dimensions={0} | all-to-all | bytes 524288 | tf_op jit(solution)/shard_map/all_to_all | solution.py:179
  72.2 23.4 %all_to_all.39 = f32[16,32,128]{2,1,0:T(8,128)S(1)} all-to-all(f32[16,32,128]{2,1,0:T(8,128)S(1)} %shard_map.62), channel_id=1, replica_groups={{0,32,64,96,128,160,192,224,256,288,320,352,384,416,448,480},{16,48,80,..., dimensions={0} | all-to-all | bytes 524288 | tf_op jit(solution)/shard_map/all_to_all | solution.py:183
  95.7 7.4 %shard_map.63 = f32[2,648,128]{2,1,0:T(8,128)S(1)} custom-call(f32[512,128]{1,0:T(8,128)S(1)} %bitcast.10), custom_call_target="tpu_custom_call" | custom-call | tf_op jit(solution)/shard_map/pallas_call | solution.py:147
  103.1 9.6 %all_to_all.40.f_ref = f32[2,648,128]{2,1,0:T(8,128)S(1)} all-to-all(f32[2,648,128]{2,1,0:T(8,128)S(1)} %shard_map.63), channel_id=1, replica_groups={{0,16},{32,48},{64,80},{96,112},{128,144},{160,176},{192,208},{224,240}..., dimensions={0} | all-to-all | bytes 1327104 | tf_op jit(solution)/shard_map/all_to_all | solution.py:188
  112.7 9.7 %all_to_all.41.n_ref = f32[16,16,128]{2,1,0:T(8,128)S(1)} all-to-all(f32[16,16,128]{2,1,0:T(8,128)S(1)} %broadcast_in_dim.8), channel_id=1, replica_groups=mesh['row'=32,'col'=16] {'col'}, dimensions={0} | all-to-all | bytes 262144 | tf_op jit(solution)/shard_map/all_to_all | solution.py:190
  122.4 4.2 %shard_map.64 = (bf16[9,224,128]{2,1,0:T(8,128)(2,1)}, f32[9,224,128]{2,1,0:T(8,128)}, f32[9,128,64]{2,1,0:T(8,128)S(1)}) custom-call(f32[16,16,128]{2,1,0:T(8,128)S(1)} %all_to_all.41.n_ref, f32[2,648,128]{2,1,0:T(8,128)S(1)} %all_to_all.40.f_ref, bf16[9,224,128]{2,1,0:T(8,128)(2,1)S(1)} %copy-done.2, f32[9,224,128]{2,1,0:T(8,128)S(1)} %copy-done.1, ...), custom_call_target="tpu_custom_call" | custom-call | tf_op jit(solution)/shard_map/pallas_call | solution.py:147
  126.6 0.9 copy.7
  (4 shorter events, 0.1 us)
Async XLA Ops:
  0.6 1.3 copy-start.2
  1.9 1.2 copy-start
  20.9 12.3 %copy-start.1 = (f32[9,224,128]{2,1,0:T(8,128)S(1)}, f32[9,224,128]{2,1,0:T(8,128)}, u32[]{:S(2)}) copy-start(f32[9,224,128]{2,1,0:T(8,128)} %m_ref.5) | copy-start | bytes 3096580

commit v2 on v1

v2 whole, which is shorter than its diff:
```python
import functools
import math

import jax
import jax.numpy as jnp
from jax import lax
from jax.experimental import pallas as pl
from jax.experimental.pallas import tpu as pltpu
from jax.sharding import PartitionSpec as P

DECAY = 1.0 - 0.95
EPS = 1e-08
HIGH = lax.Precision.HIGHEST
F32 = jnp.float32


def dot(a, b, ca=1, cb=0):
    return lax.dot_general(
        a, b, (((ca,), (cb,)), ((), ())), precision=HIGH, preferred_element_type=F32
    )


def split(x):
    hi = x.astype(jnp.bfloat16)
    return hi, (x - hi.astype(F32)).astype(jnp.bfloat16)


def project_kernel(g_hbm, m_hbm, v_hbm, b_ref, p_ref, g_ref, m_ref, v_ref, sem):
    mats, rows, _ = m_ref.shape
    half = rows // 2
    copies = [
        [
            pltpu.make_async_copy(src.at[i], dst.at[i], sem.at[i, j])
            for j, (src, dst) in enumerate(((m_hbm, m_ref), (g_hbm, g_ref), (v_hbm, v_ref)))
        ]
        for i in range(mats)
    ]
    for some in copies:
        for copy in some:
            copy.start()
    for i in range(mats):
        for copy in copies[i]:
            copy.wait()
        b = m_ref[i] + g_ref[i].astype(F32)
        b_ref[i] = b
        p = dot(b, v_ref[i], 1, 1)
        p_ref[pl.ds(i * half, half), :] = jnp.concatenate([p[:half], p[half:]], axis=1)


def sum_kernel(x_ref, o_ref):
    total = x_ref[0]
    for i in range(1, x_ref.shape[0]):
        total = total + x_ref[i]
    for i in range(o_ref.shape[0]):
        o_ref[i] = total


def pair_sum_kernel(x_ref, y_ref, o_ref):
    o_ref[...] = x_ref[...] + y_ref[...]


def products_kernel(h_ref, b_ref, p_ref, o_ref, *, slots):
    mats, rows, _ = b_ref.shape
    half = rows // 2
    rank = 64
    step = rank + rank // 2
    for s in range(slots):
        i = jnp.minimum(h_ref[0] * slots + s, mats - 1)
        b = b_ref[i]
        pp = p_ref[pl.ds(pl.multiple_of(i * half, 8), half), :]
        both = jnp.concatenate([b[:half], b[half:], pp], axis=1)
        full = dot(pp, both, 0, 0)
        y = full[:rank, :128] + full[rank:, 128:256]
        gram = full[:rank, 256 : 256 + rank] + full[rank:, 256 + rank :]
        o_ref[pl.ds(s * step, rank), :] = y
        o_ref[pl.ds(s * step + rank, rank // 2), :] = jnp.concatenate(
            [gram[: rank // 2], gram[rank // 2 :]], axis=1
        )


def factor_kernel(gy_ref, o_ref, rows_ref, *, slots):
    rank = 64
    step = rank + rank // 2
    lane = lax.broadcasted_iota(jnp.int32, (slots, 128), 1)

    def splat(row, at):
        return jnp.broadcast_to(row[:, at : at + 1], (slots, 128))

    a = []
    for i in range(rank):
        packed = gy_ref[pl.ds(rank + i % 32, slots, stride=step), :]
        if i >= 32:
            packed = pltpu.roll(packed, 64, 1)
        packed = jnp.where(lane < rank, packed, 0.0)
        a.append(jnp.where(lane == rank + i, 1.0, packed))
    size = 8
    for first in range(0, rank, size):
        e = [[splat(a[first + i], first + j) for j in range(i + 1)] for i in range(size)]
        inverse = []
        for p in range(size):
            inverse.append(1.0 / e[p][p])
            low = [None] * size
            for i in range(p + 1, size):
                low[i] = e[i][p] * inverse[p]
            for i in range(p + 1, size):
                for j in range(p + 1, i + 1):
                    e[i][j] = e[i][j] - low[i] * e[j][p]
                a[first + i] = a[first + i] - low[i] * a[first + p]
        scaled = [a[first + p] * inverse[p] for p in range(size)]
        for i in range(first + size, rank):
            terms = [splat(a[first + p], i) * scaled[p] for p in range(size)]
            while len(terms) > 1:
                terms = [terms[t] + terms[t + 1] for t in range(0, len(terms), 2)]
            a[i] = a[i] - terms[0]
        for p in range(size):
            rows_ref[pl.ds(first + p, slots, stride=rank), :] = a[first + p] * lax.rsqrt(e[p][p])
    row8 = lax.broadcasted_iota(jnp.int32, (8, 128), 0)
    table = jnp.zeros((8, 128), F32)
    zero = jnp.zeros((8, rank), F32)
    for s in range(slots):
        inv = rows_ref[pl.ds(s * rank, rank), :][:, rank:]
        xt = dot(inv, gy_ref[pl.ds(s * step, rank), :])
        n = dot(jnp.ones((8, 128), F32), xt * xt, 1, 1)
        table = jnp.where(row8 == s, jnp.concatenate([n, zero], axis=1), table)
        packed = jnp.concatenate([inv[: rank // 2], inv[rank // 2 :]], axis=1)
        for c in range(o_ref.shape[0]):
            o_ref[c, pl.ds(s * step, rank), :] = xt
            o_ref[c, pl.ds(s * step + rank, rank // 2), :] = packed
    for c in range(o_ref.shape[0]):
        o_ref[c, pl.ds(slots * step, 8), :] = table


def finish_kernel(
    n_ref, f_ref, b_ref, p_ref, u_hbm, mo_hbm, r_hbm, u_ref, mo_ref, r_ref, sem, *, slots, scale
):
    mats, rows, _ = b_ref.shape
    half = rows // 2
    rank = 64
    step = rank + rank // 2
    total = n_ref[0]
    for i in range(1, n_ref.shape[0]):
        total = total + n_ref[i]
    column = jnp.transpose(total)
    copies = []
    for i in range(mats):
        h, s = divmod(i, slots)
        xt = f_ref[h, pl.ds(s * step, rank), :]
        packed = f_ref[h, pl.ds(s * step + rank, rank // 2), :]
        inv = jnp.concatenate([packed[:, :rank], packed[:, rank:]], axis=0)
        norm = jnp.sqrt(column[:rank, h * 8 + s : h * 8 + s + 1]) + EPS
        rt = xt / norm
        r_ref[i] = rt
        w = dot(inv, jnp.concatenate([xt, rt], axis=1), 0, 0)
        wh, wl = split(w)
        pp = p_ref[pl.ds(i * half, half), :]
        p = jnp.concatenate([pp[:, :rank], pp[:, rank:]], axis=0)
        ph, pl_ = split(p)
        out = lax.dot_general(
            jnp.concatenate([ph, ph, pl_, pl_], axis=1),
            jnp.concatenate([wh, wl, wh, wl], axis=0),
            (((1,), (0,)), ((), ())),
            preferred_element_type=F32,
        )
        mo_ref[i] = b_ref[i] - DECAY * out[:, :128]
        u_ref[i] = (scale * out[:, 128:]).astype(jnp.bfloat16)
        for j, (src, dst) in enumerate(((u_ref, u_hbm), (mo_ref, mo_hbm), (r_ref, r_hbm))):
            copy = pltpu.make_async_copy(src.at[i], dst.at[i], sem.at[i, j])
            copy.start()
            copies.append(copy)
    for copy in copies:
        copy.wait()


def call(kernel, out, *args, ins=None, outs=None, scratch=(), flops=0, moved=0):
    vmem = pl.BlockSpec(memory_space=pltpu.VMEM)
    several = isinstance(out, tuple)
    outs = outs or ((vmem,) * len(out) if several else vmem)
    return pl.pallas_call(
        kernel,
        out_shape=out,
        in_specs=ins or (vmem,) * len(args),
        out_specs=outs,
        scratch_shapes=scratch,
        cost_estimate=pl.CostEstimate(flops=flops, bytes_accessed=moved, transcendentals=0),
        compiler_params=pltpu.CompilerParams(vmem_limit_bytes=32 * 1024 * 1024),
    )(*args)


def shape(*dims, dtype=F32):
    return jax.ShapeDtypeStruct(dims, dtype)


def on_device(grad, momentum, trailing_coefficients):
    mats, rows, cols = momentum.shape
    rank = trailing_coefficients.shape[2]
    n_col = lax.axis_size("col")
    n_row = lax.axis_size("row")
    core = lax.rem(lax.axis_index("row"), 2)
    near = [[(4 * h + l) * 2 + c for l in range(4)] for h in range(4) for c in range(2)]
    far = [[(4 * h + l) * 2 + c for h in range(4)] for l in range(4) for c in range(2)]
    pairs = [[2 * z, 2 * z + 1] for z in range(n_row // 2)]
    swap = [(i, i ^ 1) for i in range(n_row)]
    scale = math.sqrt(rows * n_row * cols * n_col / rank)
    slots = 5
    step = rank + rank // 2
    hbm = pl.BlockSpec(memory_space=pltpu.HBM)
    vmem = pl.BlockSpec(memory_space=pltpu.VMEM)
    smem = pl.BlockSpec(memory_space=pltpu.SMEM)

    blended, part = call(
        project_kernel,
        (shape(mats, rows, cols), shape(1024, 128)),
        grad,
        momentum,
        jnp.swapaxes(trailing_coefficients, 1, 2),
        ins=(hbm,) * 3,
        scratch=(
            pltpu.VMEM((mats, rows, cols), jnp.bfloat16),
            pltpu.VMEM((mats, rows, cols), F32),
            pltpu.VMEM((mats, rank, cols), F32),
            pltpu.SemaphoreType.DMA((mats, 3)),
        ),
    )
    pieces = lax.all_to_all(part.reshape(n_col, 64, 128), "col", 0, 0)
    summed = call(sum_kernel, shape(n_col, 64, 128), pieces)
    projected = lax.all_to_all(summed, "col", 0, 0).reshape(1024, 128)

    def products(half):
        return call(
            functools.partial(products_kernel, slots=slots),
            shape(slots * step, 128),
            half.reshape(1),
            blended,
            projected,
            ins=(smem, vmem, vmem),
            flops=5 * 10**8,
            moved=2 * 10**6,
        )

    theirs = lax.ppermute(products(1 - core), "row", swap)
    mine = products(core)
    pieces = call(pair_sum_kernel, shape(slots * step, 128), mine, theirs)
    quarter = slots * step // 4
    pieces = lax.all_to_all(
        pieces.reshape(4, quarter, 128), "row", 0, 0, axis_index_groups=near
    )
    summed = call(sum_kernel, shape(4, quarter, 128), pieces)
    pieces = lax.all_to_all(summed, "row", 0, 0, axis_index_groups=far)
    summed = call(sum_kernel, shape(4, quarter, 128), pieces)
    reduced = lax.all_to_all(summed, "row", 0, 0, axis_index_groups=near)

    factors = call(
        functools.partial(factor_kernel, slots=slots),
        shape(2, slots * step + 8, 128),
        reduced.reshape(slots * step, 128),
        scratch=(pltpu.VMEM((slots * rank, 128), F32),),
    )
    factors = lax.all_to_all(factors, "row", 0, 0, axis_index_groups=pairs)
    squares = factors[:, slots * step :, :].reshape(1, 16, 128)
    squares = lax.all_to_all(jnp.broadcast_to(squares, (n_col, 16, 128)), "col", 0, 0)

    update, momentum_next, right = call(
        functools.partial(finish_kernel, slots=slots, scale=scale),
        (
            shape(mats, rows, cols, dtype=jnp.bfloat16),
            shape(mats, rows, cols),
            shape(mats, rank, cols),
        ),
        squares,
        factors,
        blended,
        projected,
        outs=(hbm,) * 3,
        scratch=(
            pltpu.VMEM((mats, rows, cols), jnp.bfloat16),
            pltpu.VMEM((mats, rows, cols), F32),
            pltpu.VMEM((mats, rank, cols), F32),
            pltpu.SemaphoreType.DMA((mats, 3)),
        ),
    )
    return update, momentum_next, jnp.swapaxes(right, 1, 2)


def solution(mesh):
    return jax.shard_map(
        on_device,
        mesh=mesh,
        in_specs=(P(None, "row", "col"), P(None, "row", "col"), P(None, "col", None)),
        out_specs=(P(None, "row", "col"), P(None, "row", "col"), P(None, "col", None)),
        check_vma=False,
    )
```

time: 128 us -> 128 us (level)
  blocking collectives: 109 us -> 86.4 us
  starting transfers between devices: 0 us -> 9.86 us
  waiting for transfers between devices: 0 us -> 8.91 us
  Pallas kernels: 14.6 us -> 18.4 us
    all_to_all x4 -> x3, blocking collectives: 72.9 us -> 51.2 us  [the longest x1 27.3 us: on_device(): pieces = lax.all_to_all(summed, 'row', 0, 0, axis_index_groups=far)]
    all_to_all x0 -> x1, waiting for transfers between devices: none -> 8.91 us  [on_device(): projected = lax.all_to_all(summed, 'col', 0, 0).reshape(1024, 128)]
    ppermute x0 -> x1, starting transfers between devices: none -> 6.28 us  [on_device(): theirs = lax.ppermute(products(1 - core), 'row', swap)]
    pallas_call x7 -> x9, Pallas kernels: 14.6 us -> 18.4 us  [call(): pl.pallas_call(kernel, out_shape=out, in_specs=ins or (vmem,) * len(args)...]
    all_to_all x0 -> x1, starting transfers between devices: none -> 3.57 us  [on_device(): projected = lax.all_to_all(summed, 'col', 0, 0).reshape(1024, 128)]
    unnamed x7 -> x6, local copies, waits for them, and re-layouts: 2.47 us -> 3.21 us
  transfers between devices with their start and end apart: 0 -> 2, of which waited for: 0 -> 1; matrix products, arithmetic and copies ran while one was open for 0% -> 0% of each run, Pallas kernels for 0% -> 1%
where the time goes in v2:
time: 128 us; the launch traced here: 127 us
  blocking collectives  86.4 us (68%)
  Pallas kernels  18.4 us (14%)
  starting transfers between devices  9.86 us (8%)
  waiting for transfers between devices  8.91 us (7%)
  local copies, waits for them, and re-layouts  3.23 us (3%)
    all_to_all x1, blocking collectives, on_device(): pieces = lax.all_to_all(summed, 'row', 0, 0, axis_index_groups=far)  27.3 us
    pallas_call x9, Pallas kernels, call(): pl.pallas_call(kernel, out_shape=out, in_specs=ins or (vmem,) * len(args)...  18.4 us
    all_to_all x1, blocking collectives, on_device(): pieces = lax.all_to_all(part.reshape(n_col, 64, 128), 'col', 0, 0)  16.6 us
    all_to_all x1, blocking collectives, on_device(): lax.all_to_all(pieces.reshape(4, quarter, 128), 'row', 0, 0, axis_index_g...  12.2 us
    all_to_all x1, blocking collectives, on_device(): reduced = lax.all_to_all(summed, 'row', 0, 0, axis_index_groups=near)  11.7 us
    all_to_all x1, blocking collectives, on_device(): lax.all_to_all(jnp.broadcast_to(squares, (n_col, 16, 128)), 'col', 0, 0)  9.83 us
    all_to_all x1, waiting for transfers between devices, on_device(): projected = lax.all_to_all(summed, 'col', 0, 0).reshape(1024, 128)  8.91 us
    all_to_all x1, blocking collectives, on_device(): factors = lax.all_to_all(factors, 'row', 0, 0, axis_index_groups=pairs)  8.8 us
  transfers between devices with their start and end apart: 2, of which 1 were waited for; matrix products, arithmetic and copies ran while one was open for 0% of the time, Pallas kernels for 1%

profile of v2, /device:TPU:1, one launch (start us, length us, event | category | flops | bytes accessed | tf_op | source)
XLA Modules:
  0.0 127.4 jit_solution(17837629814614857769)
XLA Ops:
  0.6 0.0 copy-start
  0.6 1.2 copy-done
  1.9 0.0 copy-start.1
  1.9 1.0 copy-done.1
  2.9 0.0 copy-start.2
  2.9 1.0 copy-done.2
  3.9 6.0 %shard_map.58 = (f32[9,224,128]{2,1,0:T(8,128)S(1)}, f32[1024,128]{1,0:T(8,128)S(1)}) custom-call(bf16[9,224,128]{2,1,0:T(8,128)(2,1)S(1)} %copy-done.1, f32[9,224,128]{2,1,0:T(8,128)S(1)} %copy-done, f32[9,64,128]{2,1,0:T(8,128)S(1)} %bitcast.16), custom_call_target="tpu_custom_call" | custom-call | tf_op jit(solution)/shard_map/pallas_call | solution.py:178
  9.8 16.6 %all_to_all.35.x_ref = f32[16,64,128]{2,1,0:T(8,128)S(1)} all-to-all(f32[16,64,128]{2,1,0:T(8,128)S(1)} %bitcast.15), channel_id=1, replica_groups=mesh['row'=32,'col'=16] {'col'}, dimensions={0} | all-to-all | bytes 1048576 | tf_op jit(solution)/shard_map/all_to_all | solution.py:224
  26.4 0.9 shard_map.59
  27.3 3.6 %all-to-all-start.1 = ((f32[16,64,128]{2,1,0:T(8,128)}), f32[16,64,128]{2,1,0:T(8,128)S(1)}, u32[]{:S(2)}, u32[]{:S(2)}) async-start(f32[16,64,128]{2,1,0:T(8,128)} %shard_map.59), calls=%async_computation.1 | async-start | bytes 1048576 | tf_op jit(solution)/shard_map/all_to_all | solution.py:226
  30.9 8.9 %all-to-all-done.1 = f32[16,64,128]{2,1,0:T(8,128)S(1)} async-done(((f32[16,64,128]{2,1,0:T(8,128)}), f32[16,64,128]{2,1,0:T(8,128)S(1)}, u32[]{:S(2)}, u32[]{:S(2)}) %all-to-all-start.1) | async-done | bytes 524320 | tf_op jit(solution)/shard_map/all_to_all | solution.py:226
  39.8 1.1 shard_map.61
  40.9 6.3 %collective-permute-start = (f32[480,128]{1,0:T(8,128)S(1)}, f32[480,128]{1,0:T(8,128)S(1)}, u32[]{:S(2)}, u32[]{:S(2)}) collective-permute-start(f32[480,128]{1,0:T(8,128)S(1)} %shard_map.61), channel_id=1, source_target_pairs={{0,16},{16,0},{32,48},{48,32},{64,80},{80,64},{96,112},{112,96},{1... | collective-permute-start | bytes 737288 | tf_op jit(solution)/shard_map/ppermute | solution.py:240
  47.2 1.1 shard_map.60.x_ref
  48.3 0.0 collective-permute-done.y_ref
  48.3 12.2 %all_to_all.36.x_ref = f32[4,120,128]{2,1,0:T(8,128)S(1)} all-to-all(f32[4,120,128]{2,1,0:T(8,128)S(1)} %bitcast.13), channel_id=1, replica_groups={{0,32,64,96},{16,48,80,112},{128,160,192,224},{144,176,208,240},{256,28..., dimensions={0} | all-to-all | bytes 491520 | tf_op jit(solution)/shard_map/all_to_all | solution.py:244
  60.5 27.3 %all_to_all.37.x_ref = f32[4,120,128]{2,1,0:T(8,128)S(1)} all-to-all(f32[4,120,128]{2,1,0:T(8,128)S(1)} %shard_map.63), channel_id=1, replica_groups={{0,128,256,384},{16,144,272,400},{32,160,288,416},{48,176,304,432},{64,..., dimensions={0} | all-to-all | bytes 491520 | tf_op jit(solution)/shard_map/all_to_all | solution.py:248
  87.9 11.7 %all_to_all.38 = f32[4,120,128]{2,1,0:T(8,128)S(1)} all-to-all(f32[4,120,128]{2,1,0:T(8,128)S(1)} %shard_map.64), channel_id=1, replica_groups={{0,32,64,96},{16,48,80,112},{128,160,192,224},{144,176,208,240},{256,28..., dimensions={0} | all-to-all | bytes 491520 | tf_op jit(solution)/shard_map/all_to_all | solution.py:250
  99.5 5.3 %shard_map.65 = f32[2,488,128]{2,1,0:T(8,128)S(1)} custom-call(f32[480,128]{1,0:T(8,128)S(1)} %bitcast.14), custom_call_target="tpu_custom_call" | custom-call | tf_op jit(solution)/shard_map/pallas_call | solution.py:178
  104.8 8.8 %all_to_all.39.f_ref = f32[2,488,128]{2,1,0:T(8,128)S(1)} all-to-all(f32[2,488,128]{2,1,0:T(8,128)S(1)} %shard_map.65), channel_id=1, replica_groups={{0,16},{32,48},{64,80},{96,112},{128,144},{160,176},{192,208},{224,240}..., dimensions={0} | all-to-all | bytes 999424 | tf_op jit(solution)/shard_map/all_to_all | solution.py:258
  113.7 9.8 %all_to_all.40.n_ref = f32[16,16,128]{2,1,0:T(8,128)S(1)} all-to-all(f32[16,16,128]{2,1,0:T(8,128)S(1)} %broadcast_in_dim.8), channel_id=1, replica_groups=mesh['row'=32,'col'=16] {'col'}, dimensions={0} | all-to-all | bytes 262144 | tf_op jit(solution)/shard_map/all_to_all | solution.py:260
  123.5 4.0 %shard_map.66 = (bf16[9,224,128]{2,1,0:T(8,128)(2,1)}, f32[9,224,128]{2,1,0:T(8,128)}, f32[9,64,128]{2,1,0:T(8,128)}) custom-call(f32[16,16,128]{2,1,0:T(8,128)S(1)} %all_to_all.40.n_ref, f32[2,488,128]{2,1,0:T(8,128)S(1)} %all_to_all.39.f_ref, f32[9,224,128]{2,1,0:T(8,128)S(1)} %get-tuple-element.8.b_ref, f32[1024,128]{1,0:T(8,128)S(1)} %bitcast.12), custom_call_target="tpu_custom_call" | custom-call | tf_op jit(solution)/shard_map/pallas_call | solution.py:178
  (5 shorter events, 0.1 us)
Async XLA Ops:
  0.6 1.2 copy-start
  1.9 1.0 copy-start.1
  2.9 1.0 copy-start.2
  27.3 12.5 %all-to-all-start.1 = ((f32[16,64,128]{2,1,0:T(8,128)}), f32[16,64,128]{2,1,0:T(8,128)S(1)}, u32[]{:S(2)}, u32[]{:S(2)}) async-start(f32[16,64,128]{2,1,0:T(8,128)} %shard_map.59), calls=%async_computation.1 | async-start | bytes 1048576 | tf_op jit(solution)/shard_map/all_to_all | solution.py:226
  40.9 7.4 %collective-permute-start = (f32[480,128]{1,0:T(8,128)S(1)}, f32[480,128]{1,0:T(8,128)S(1)}, u32[]{:S(2)}, u32[]{:S(2)}) collective-permute-start(f32[480,128]{1,0:T(8,128)S(1)} %shard_map.61), channel_id=1, source_target_pairs={{0,16},{16,0},{32,48},{48,32},{64,80},{80,64},{96,112},{112,96},{1... | collective-permute-start | bytes 737288 | tf_op jit(solution)/shard_map/ppermute | solution.py:240

commit v3 on v0

v3 whole, which is shorter than its diff:
```python
import functools
import math

import jax
import jax.numpy as jnp
from jax import lax
from jax.experimental import pallas as pl
from jax.experimental.pallas import tpu as pltpu
from jax.sharding import PartitionSpec as P

DECAY = 1.0 - 0.95
EPS = 1e-08
F32 = jnp.float32
BF16 = jnp.bfloat16
ORDER = ((0, 0), (0, 1), (1, 0), (1, 1), (0, 2), (2, 0))


def parts(x, count):
    out = []
    for _ in range(count):
        out.append(x.astype(BF16))
        x = x - out[-1].astype(F32)
    return out


def dot(a, b, ca=1, cb=0, terms=6):
    count = 3 if terms > 4 else 2
    a, b = parts(a, count), parts(b, count)
    return lax.dot_general(
        jnp.concatenate([a[i] for i, _ in ORDER[:terms]], axis=ca),
        jnp.concatenate([b[j] for _, j in ORDER[:terms]], axis=cb),
        (((ca,), (cb,)), ((), ())),
        preferred_element_type=F32,
    )


def project_kernel(b_ref, v_ref, p_ref):
    mats, rows, _ = b_ref.shape
    half = rows // 2
    for i in range(mats):
        p = dot(b_ref[i], v_ref[i], 1, 1, 3)
        p_ref[pl.ds(i * half, half), :] = jnp.concatenate([p[:half], p[half:]], axis=1)


def sum_kernel(x_ref, o_ref):
    total = x_ref[0]
    for i in range(1, x_ref.shape[0]):
        total = total + x_ref[i]
    for i in range(o_ref.shape[0]):
        o_ref[i] = total


def pair_sum_kernel(x_ref, y_ref, o_ref):
    o_ref[...] = x_ref[...] + y_ref[...]


def products_kernel(h_ref, b_ref, p_ref, o_ref, *, slots):
    mats, rows, _ = b_ref.shape
    half = rows // 2
    rank = 64
    step = rank + rank // 2
    for s in range(slots):
        i = jnp.minimum(h_ref[0] * slots + s, mats - 1)
        b = b_ref[i]
        pp = p_ref[pl.ds(pl.multiple_of(i * half, 8), half), :]
        full = dot(pp, jnp.concatenate([b[:half], b[half:], pp], axis=1), 0, 0)
        gram = full[:rank, 256 : 256 + rank] + full[rank:, 256 + rank :]
        o_ref[pl.ds(s * step, rank), :] = full[:rank, :128] + full[rank:, 128:256]
        o_ref[pl.ds(s * step + rank, rank // 2), :] = jnp.concatenate(
            [gram[: rank // 2], gram[rank // 2 :]], axis=1
        )


def factor_kernel(gy_ref, o_ref, a_ref, h_ref, *, slots):
    rank = 64
    size = 16
    step = rank + rank // 2
    row = lax.broadcasted_iota(jnp.int32, (rank, rank), 0)
    lane = lax.broadcasted_iota(jnp.int32, (rank, rank), 1)
    eye = jnp.where(lane == row, 1.0, 0.0).astype(F32)
    for s in range(slots):
        packed = gy_ref[pl.ds(s * step + rank, rank // 2), :]
        gram = jnp.concatenate([packed[:, :rank], packed[:, rank:]], axis=0)
        a_ref[pl.ds(s * rank, rank), :] = jnp.concatenate([gram, eye], axis=1)
    for first in range(0, rank, size):
        a = [a_ref[pl.ds(first + p, slots, stride=rank), :] for p in range(size)]
        e = [
            [
                jnp.broadcast_to(a[i][:, first + j : first + j + 1], (slots, 128))
                for j in range(i + 1)
            ]
            for i in range(size)
        ]
        for p in range(size):
            root = lax.rsqrt(e[p][p])
            root = root * (1.5 - 0.5 * e[p][p] * root * root)
            a[p] = a[p] * root
            low = [None] * size
            for i in range(p + 1, size):
                low[i] = e[i][p] * root
            for i in range(p + 1, size):
                for j in range(p + 1, i + 1):
                    e[i][j] = e[i][j] - low[i] * low[j]
                a[i] = a[i] - low[i] * a[p]
            h_ref[pl.ds(first + p, slots, stride=rank), :] = a[p]
        left = rank - first - size
        if left:
            for s in range(slots):
                h = h_ref[pl.ds(s * rank + first, size), :]
                at = pl.ds(s * rank + first + size, left)
                a_ref[at, :] = a_ref[at, :] - dot(h[:, first + size : rank], h, 0, 0)
    row8 = lax.broadcasted_iota(jnp.int32, (8, 128), 0)
    table = jnp.zeros((8, 128), F32)
    zero = jnp.zeros((8, rank), F32)
    for s in range(slots):
        inv = h_ref[pl.ds(s * rank, rank), :][:, rank:]
        xt = dot(inv, gy_ref[pl.ds(s * step, rank), :])
        squares = dot(jnp.ones((8, 128), F32), xt * xt, 1, 1)
        table = jnp.where(row8 == s, jnp.concatenate([squares, zero], axis=1), table)
        o_ref[pl.ds(s * step, rank), :] = xt
        o_ref[pl.ds(s * step + rank, rank // 2), :] = jnp.concatenate(
            [inv[: rank // 2], inv[rank // 2 :]], axis=1
        )
    o_ref[pl.ds(slots * step, 8), :] = table


def retain_kernel(core_ref, mine_ref, theirs_ref, b_ref, p_ref, mo_ref, q_ref, *, slots):
    mats, rows, _ = b_ref.shape
    half = rows // 2
    rank = 64
    step = rank + rank // 2
    core = core_ref[0]
    for i in range(mats):
        h, s = divmod(i, slots)
        at = pl.ds(s * step, step)
        factor = jnp.where(core == h, mine_ref[at, :], theirs_ref[at, :])
        xt, packed = factor[:rank], factor[rank:]
        inv = jnp.concatenate([packed[:, :rank], packed[:, rank:]], axis=0)
        pp = p_ref[pl.ds(i * half, half), :]
        p = jnp.concatenate([pp[:, :rank], pp[:, rank:]], axis=0)
        qh, ql = parts(dot(p, inv, 1, 1, 4), 2)
        q = jnp.concatenate([qh, qh, ql, ql], axis=1)
        q_ref[i] = q
        xh, xl = parts(xt, 2)
        low_rank = jnp.dot(
            q, jnp.concatenate([xh, xl, xh, xl], axis=0), preferred_element_type=F32
        )
        mo_ref[i] = b_ref[i] - DECAY * low_rank


def update_kernel(
    core_ref, n_ref, mine_ref, theirs_ref, q_ref, u_ref, r_ref, *, slots, scale
):
    mats = q_ref.shape[0]
    rank = 64
    step = rank + rank // 2
    core = core_ref[0]
    total = n_ref[0]
    for i in range(1, n_ref.shape[0]):
        total = total + n_ref[i]
    inverse = 1.0 / (jnp.sqrt(jnp.transpose(total)) + EPS)
    for i in range(mats):
        h, s = divmod(i, slots)
        at = pl.ds(s * step, rank)
        xt = jnp.where(core == h, mine_ref[at, :], theirs_ref[at, :])
        rt = xt * jnp.where(core == h, inverse[:rank, s : s + 1], inverse[:rank, 8 + s : 9 + s])
        r_ref[i] = rt
        rh, rl = parts(scale * rt, 2)
        u_ref[i] = jnp.dot(
            q_ref[i], jnp.concatenate([rh, rl, rh, rl], axis=0), preferred_element_type=F32
        ).astype(BF16)


def call(kernel, out, *args, scalar=False, scratch=(), flops=0, moved=0):
    vmem = pl.BlockSpec(memory_space=pltpu.VMEM)
    first = pl.BlockSpec(memory_space=pltpu.SMEM) if scalar else vmem
    return pl.pallas_call(
        kernel,
        out_shape=out,
        in_specs=(first,) + (vmem,) * (len(args) - 1),
        out_specs=(vmem,) * len(out) if isinstance(out, tuple) else vmem,
        scratch_shapes=scratch,
        cost_estimate=pl.CostEstimate(flops=flops, bytes_accessed=moved, transcendentals=0),
        compiler_params=pltpu.CompilerParams(vmem_limit_bytes=32 * 1024 * 1024),
    )(*args)


def shape(*dims, dtype=F32):
    return jax.ShapeDtypeStruct(dims, dtype)


def on_device(grad, momentum, trailing_coefficients):
    mats, rows, cols = momentum.shape
    rank = trailing_coefficients.shape[2]
    n_col = lax.axis_size("col")
    n_row = lax.axis_size("row")
    core = lax.rem(lax.axis_index("row"), 2)
    here = core.reshape(1)
    near = [[(4 * h + l) * 2 + c for l in range(4)] for h in range(4) for c in range(2)]
    far = [[(4 * h + l) * 2 + c for h in range(4)] for l in range(4) for c in range(2)]
    swap = [(i, i ^ 1) for i in range(n_row)]
    scale = math.sqrt(rows * n_row * cols * n_col / rank)
    slots = 5
    step = rank + rank // 2
    work = dict(flops=5 * 10**8, moved=2 * 10**6)

    blended = momentum + grad.astype(F32)
    part = call(
        project_kernel, shape(1024, 128), blended, jnp.swapaxes(trailing_coefficients, 1, 2)
    )
    pieces = lax.all_to_all(part.reshape(n_col, 64, 128), "col", 0, 0)
    summed = call(sum_kernel, shape(n_col, 64, 128), pieces)
    projected = lax.all_to_all(summed, "col", 0, 0).reshape(1024, 128)

    def products(half):
        return call(
            functools.partial(products_kernel, slots=slots),
            shape(slots * step, 128),
            half,
            blended,
            projected,
            scalar=True,
            **work,
        )

    theirs = lax.ppermute(products(1 - here), "row", swap)
    mine = products(here)
    pieces = call(pair_sum_kernel, shape(slots * step, 128), mine, theirs)
    quarter = slots * step // 4
    pieces = lax.all_to_all(
        pieces.reshape(4, quarter, 128), "row", 0, 0, axis_index_groups=near
    )
    summed = call(sum_kernel, shape(4, quarter, 128), pieces)
    pieces = lax.all_to_all(summed, "row", 0, 0, axis_index_groups=far)
    summed = call(sum_kernel, shape(4, quarter, 128), pieces)
    reduced = lax.all_to_all(summed, "row", 0, 0, axis_index_groups=near)

    mine = call(
        functools.partial(factor_kernel, slots=slots),
        shape(slots * step + 8, 128),
        reduced.reshape(slots * step, 128),
        scratch=(pltpu.VMEM((slots * rank, 128), F32),) * 2,
    )
    theirs = lax.ppermute(mine, "row", swap)
    squares = jnp.concatenate([mine[slots * step :], theirs[slots * step :]], axis=0)
    squares = lax.all_to_all(
        jnp.broadcast_to(squares[None], (n_col, 16, 128)), "col", 0, 0
    )
    momentum_next, orthonormal = call(
        functools.partial(retain_kernel, slots=slots),
        (shape(mats, rows, cols), shape(mats, rows, 4 * rank, dtype=BF16)),
        here,
        mine,
        theirs,
        blended,
        projected,
        scalar=True,
        **work,
    )
    update, right = call(
        functools.partial(update_kernel, slots=slots, scale=scale),
        (shape(mats, rows, cols, dtype=BF16), shape(mats, rank, cols)),
        here,
        squares,
        mine,
        theirs,
        orthonormal,
        scalar=True,
    )
    return update, momentum_next, jnp.swapaxes(right, 1, 2)


def solution(mesh):
    return jax.shard_map(
        on_device,
        mesh=mesh,
        in_specs=(P(None, "row", "col"), P(None, "row", "col"), P(None, "col", None)),
        out_specs=(P(None, "row", "col"), P(None, "row", "col"), P(None, "col", None)),
        check_vma=False,
    )
```

time: 685 us -> 115 us (0.17)
  waiting for transfers between devices: 516 us -> 14.6 us
  other arithmetic: 98.6 us -> 1.49 us
  blocking collectives: 33.7 us -> 66.8 us
  starting transfers between devices: 0.12 us -> 20.3 us
  matrix products: 15 us -> 0 us
  between operations: 13.9 us -> 0.72 us
  Pallas kernels: 0 us -> 10.3 us
    psum x3 -> x0, waiting for transfers between devices: 516 us -> none  [the longest x1 199 us: on_device(): reduced_gram_matrix = lax.psum(shard_gram_matrix, 'row')]
    another operation x7 -> x0, other arithmetic: 97.3 us -> none  [the longest x4 52.9 us: on_device(): lower_factor = jnp.linalg.cholesky(reduced_gram_matrix)]
    all_to_all x0 -> x4, blocking collectives: none -> 66.8 us  [the longest x1 27.3 us: on_device(): pieces = lax.all_to_all(summed, 'row', 0, 0, axis_index_groups=far)]
    psum x1 -> x0, blocking collectives: 33.7 us -> none  [on_device(): lax.psum(jnp.sum(cross_product_matrix * cross_product_matrix, axis=1), 'c...]
    dot_general x5 -> x0, matrix products: 14.3 us -> none  [the longest x1 4.18 us: on_device(): jnp.einsum('ulv,uvw->ulw', blending_velocity, trailing_coefficients, prec...]
    all_to_all x0 -> x2, waiting for transfers between devices: none -> 13.3 us  [the longest x1 8.91 us: on_device(): projected = lax.all_to_all(summed, 'col', 0, 0).reshape(1024, 128)]
    ppermute x0 -> x2, starting transfers between devices: none -> 13.2 us  [the longest x1 6.93 us: on_device(): theirs = lax.ppermute(mine, 'row', swap)]
    pallas_call x0 -> x10, Pallas kernels: none -> 10.3 us  [call(): pl.pallas_call(kernel, out_shape=out, in_specs=(first,) + (vmem,) * (len(...]
  transfers between devices with their start and end apart: 3 -> 4, of which waited for: 3 -> 4; matrix products, arithmetic and copies ran while one was open for 0% -> 0% of each run, Pallas kernels for 0% -> 3%
where the time goes in v3:
time: 115 us
  blocking collectives  66.8 us (58%)
  starting transfers between devices  20.3 us (18%)
  waiting for transfers between devices  14.6 us (13%)
  Pallas kernels  10.3 us (9%)
  other arithmetic  1.49 us (1%)
    all_to_all x1, blocking collectives, on_device(): pieces = lax.all_to_all(summed, 'row', 0, 0, axis_index_groups=far)  27.3 us
    all_to_all x1, blocking collectives, on_device(): pieces = lax.all_to_all(part.reshape(n_col, 64, 128), 'col', 0, 0)  16.6 us
    all_to_all x1, blocking collectives, on_device(): lax.all_to_all(pieces.reshape(4, quarter, 128), 'row', 0, 0, axis_index_g...  12.2 us
    all_to_all x1, blocking collectives, on_device(): reduced = lax.all_to_all(summed, 'row', 0, 0, axis_index_groups=near)  10.8 us
    pallas_call x10, Pallas kernels, call(): pl.pallas_call(kernel, out_shape=out, in_specs=(first,) + (vmem,) * (len(...  10.3 us
    all_to_all x1, waiting for transfers between devices, on_device(): projected = lax.all_to_all(summed, 'col', 0, 0).reshape(1024, 128)  8.91 us
    ppermute x1, starting transfers between devices, on_device(): theirs = lax.ppermute(mine, 'row', swap)  6.93 us
    ppermute x1, starting transfers between devices, on_device(): theirs = lax.ppermute(products(1 - here), 'row', swap)  6.27 us
  transfers between devices with their start and end apart: 4, of which 4 were waited for; matrix products, arithmetic and copies ran while one was open for 0% of the time, Pallas kernels for 3%

profile of v3, /device:TPU:1, one launch (start us, length us, event | category | flops | bytes accessed | tf_op | source)
XLA Modules:
  0.0 114.9 jit_solution(4514756135603508306)
XLA Ops:
  0.6 0.0 copy-start
  0.6 1.5 %convert_add_fusion.b_ref = f32[9,224,128]{2,1,0:T(8,128)S(1)} fusion(f32[9,224,128]{2,1,0:T(8,128)} %param.4, bf16[9,224,128]{2,1,0:T(8,128)(2,1)} %param.3), kind=kLoop, calls=%fused_computation | loop fusion | flops 516096 | bytes 2580480 | tf_op jit(solution)/shard_map/add | solution.py:207
  2.1 0.0 copy-done
  2.1 0.6 shard_map.58
  2.8 16.6 %all_to_all.30.x_ref = f32[16,64,128]{2,1,0:T(8,128)S(1)} all-to-all(f32[16,64,128]{2,1,0:T(8,128)S(1)} %bitcast.10), channel_id=1, replica_groups=mesh['row'=32,'col'=16] {'col'}, dimensions={0} | all-to-all | bytes 1048576 | tf_op jit(solution)/shard_map/all_to_all | solution.py:211
  19.4 0.9 shard_map.59
  20.2 3.6 %all-to-all-start.1 = ((f32[16,64,128]{2,1,0:T(8,128)}), f32[16,64,128]{2,1,0:T(8,128)S(1)}, u32[]{:S(2)}, u32[]{:S(2)}) async-start(f32[16,64,128]{2,1,0:T(8,128)} %shard_map.59), calls=%async_computation.1 | async-start | bytes 1048576 | tf_op jit(solution)/shard_map/all_to_all | solution.py:213
  23.8 8.9 %all-to-all-done.1 = f32[16,64,128]{2,1,0:T(8,128)S(1)} async-done(((f32[16,64,128]{2,1,0:T(8,128)}), f32[16,64,128]{2,1,0:T(8,128)S(1)}, u32[]{:S(2)}, u32[]{:S(2)}) %all-to-all-start.1) | async-done | bytes 524320 | tf_op jit(solution)/shard_map/all_to_all | solution.py:213
  32.7 0.9 shard_map.61
  33.6 6.3 %collective-permute-start = (f32[480,128]{1,0:T(8,128)S(1)}, f32[480,128]{1,0:T(8,128)S(1)}, u32[]{:S(2)}, u32[]{:S(2)}) collective-permute-start(f32[480,128]{1,0:T(8,128)S(1)} %shard_map.61), channel_id=1, source_target_pairs={{0,16},{16,0},{32,48},{48,32},{64,80},{80,64},{96,112},{112,96},{1... | collective-permute-start | bytes 737288 | tf_op jit(solution)/shard_map/ppermute | solution.py:226
  39.9 0.9 shard_map.60.x_ref
  40.7 0.2 collective-permute-done.y_ref
  41.0 12.2 %all_to_all.31.x_ref = f32[4,120,128]{2,1,0:T(8,128)S(1)} all-to-all(f32[4,120,128]{2,1,0:T(8,128)S(1)} %bitcast.11), channel_id=1, replica_groups={{0,32,64,96},{16,48,80,112},{128,160,192,224},{144,176,208,240},{256,28..., dimensions={0} | all-to-all | bytes 491520 | tf_op jit(solution)/shard_map/all_to_all | solution.py:230
  53.2 27.3 %all_to_all.32.x_ref = f32[4,120,128]{2,1,0:T(8,128)S(1)} all-to-all(f32[4,120,128]{2,1,0:T(8,128)S(1)} %shard_map.63), channel_id=1, replica_groups={{0,128,256,384},{16,144,272,400},{32,160,288,416},{48,176,304,432},{64,..., dimensions={0} | all-to-all | bytes 491520 | tf_op jit(solution)/shard_map/all_to_all | solution.py:234
  80.6 10.8 %all_to_all.33 = f32[4,120,128]{2,1,0:T(8,128)S(1)} all-to-all(f32[4,120,128]{2,1,0:T(8,128)S(1)} %shard_map.64), channel_id=1, replica_groups={{0,32,64,96},{16,48,80,112},{128,160,192,224},{144,176,208,240},{256,28..., dimensions={0} | all-to-all | bytes 491520 | tf_op jit(solution)/shard_map/all_to_all | solution.py:236
  91.3 3.2 %shard_map.65.mine_ref = f32[488,128]{1,0:T(8,128)S(1)} custom-call(f32[480,128]{1,0:T(8,128)S(1)} %bitcast.12), custom_call_target="tpu_custom_call" | custom-call | tf_op jit(solution)/shard_map/pallas_call | solution.py:177
  94.5 6.9 %collective-permute-start.1 = (f32[488,128]{1,0:T(8,128)S(1)}, f32[488,128]{1,0:T(8,128)S(1)}, u32[]{:S(2)}, u32[]{:S(2)}) collective-permute-start(f32[488,128]{1,0:T(8,128)S(1)} %shard_map.65.mine_ref), channel_id=1, source_target_pairs={{0,16},{16,0},{32,48},{48,32},{64,80},{80,64},{96,112},{112,96},{1... | collective-permute-start | bytes 749576 | tf_op jit(solution)/shard_map/ppermute | solution.py:244
  101.4 1.1 collective-permute-done.1.theirs_ref
  102.6 0.7 broadcast_in_dim.2
  103.2 3.5 %all-to-all-start.5 = ((f32[16,16,128]{2,1,0:T(8,128)}), f32[16,16,128]{2,1,0:T(8,128)S(1)}, u32[]{:S(2)}, u32[]{:S(2)}) async-start(f32[16,16,128]{2,1,0:T(8,128)} %broadcast_in_dim.2), calls=%async_computation.5 | async-start | bytes 262144 | tf_op jit(solution)/shard_map/all_to_all | solution.py:246
  106.7 2.4 %shard_map.66 = (f32[9,224,128]{2,1,0:T(8,128)}, bf16[9,224,256]{2,1,0:T(8,128)(2,1)S(1)}) custom-call(s32[1]{0:T(128)} %bitcast.h_ref.core_ref, f32[488,128]{1,0:T(8,128)S(1)} %shard_map.65.mine_ref, f32[488,128]{1,0:T(8,128)S(1)} %collective-permute-done.1.theirs_ref, f32[9,224,128]{2,1,0:T(8,128)S(1)} %convert_add_fusion.b_ref, f32[1024,128]{1,0:T(8,128)S(1)} %bitcast.9), custom_call_target="tpu_custom_call" | custom-call | flops 500000000 | bytes 2000000 | tf_op jit(solution)/shard_map/pallas_call | solution.py:177
  109.1 4.4 %all-to-all-done.5.n_ref = f32[16,16,128]{2,1,0:T(8,128)S(1)} async-done(((f32[16,16,128]{2,1,0:T(8,128)}), f32[16,16,128]{2,1,0:T(8,128)S(1)}, u32[]{:S(2)}, u32[]{:S(2)}) %all-to-all-start.5) | async-done | bytes 131104 | tf_op jit(solution)/shard_map/all_to_all | solution.py:246
  113.5 1.5 %shard_map.67 = (bf16[9,224,128]{2,1,0:T(8,128)(2,1)}, f32[9,64,128]{2,1,0:T(8,128)}) custom-call(s32[1]{0:T(128)} %bitcast.h_ref.core_ref, f32[16,16,128]{2,1,0:T(8,128)S(1)} %all-to-all-done.5.n_ref, f32[488,128]{1,0:T(8,128)S(1)} %shard_map.65.mine_ref, f32[488,128]{1,0:T(8,128)S(1)} %collective-permute-done.1.theirs_ref, ...), custom_call_target="tpu_custom_call" | custom-call | tf_op jit(solution)/shard_map/pallas_call | solution.py:177
  (6 shorter events, 0.1 us)
Async XLA Ops:
  0.6 1.5 %copy-start = (f32[9,128,64]{1,2,0:T(8,128)S(1)}, f32[9,128,64]{1,2,0:T(8,128)}, u32[]{:S(2)}) copy-start(f32[9,128,64]{1,2,0:T(8,128)} %param.5) | copy-start | bytes 884740
  20.2 12.5 %all-to-all-start.1 = ((f32[16,64,128]{2,1,0:T(8,128)}), f32[16,64,128]{2,1,0:T(8,128)S(1)}, u32[]{:S(2)}, u32[]{:S(2)}) async-start(f32[16,64,128]{2,1,0:T(8,128)} %shard_map.59), calls=%async_computation.1 | async-start | bytes 1048576 | tf_op jit(solution)/shard_map/all_to_all | solution.py:213
  33.6 7.4 %collective-permute-start = (f32[480,128]{1,0:T(8,128)S(1)}, f32[480,128]{1,0:T(8,128)S(1)}, u32[]{:S(2)}, u32[]{:S(2)}) collective-permute-start(f32[480,128]{1,0:T(8,128)S(1)} %shard_map.61), channel_id=1, source_target_pairs={{0,16},{16,0},{32,48},{48,32},{64,80},{80,64},{96,112},{112,96},{1... | collective-permute-start | bytes 737288 | tf_op jit(solution)/shard_map/ppermute | solution.py:226
  94.5 8.1 %collective-permute-start.1 = (f32[488,128]{1,0:T(8,128)S(1)}, f32[488,128]{1,0:T(8,128)S(1)}, u32[]{:S(2)}, u32[]{:S(2)}) collective-permute-start(f32[488,128]{1,0:T(8,128)S(1)} %shard_map.65.mine_ref), channel_id=1, source_target_pairs={{0,16},{16,0},{32,48},{48,32},{64,80},{80,64},{96,112},{112,96},{1... | collective-permute-start | bytes 749576 | tf_op jit(solution)/shard_map/ppermute | solution.py:244
  103.2 10.2 %all-to-all-start.5 = ((f32[16,16,128]{2,1,0:T(8,128)}), f32[16,16,128]{2,1,0:T(8,128)S(1)}, u32[]{:S(2)}, u32[]{:S(2)}) async-start(f32[16,16,128]{2,1,0:T(8,128)} %broadcast_in_dim.2), calls=%async_computation.5 | async-start | bytes 262144 | tf_op jit(solution)/shard_map/all_to_all | solution.py:246

commit v4 on v3

--- a/solution.py
+++ b/solution.py
@@ -54,33 +54,89 @@
     o_ref[...] = x_ref[...] + y_ref[...]
 
 
-def products_kernel(h_ref, b_ref, p_ref, o_ref, *, slots):
+RANK = 64
+FOUR = 4
+SHARED = FOUR * RANK
+SQUARES = SHARED + RANK // 2
+LAST = SQUARES + 2 * (RANK // 2)
+HALF_ROWS = LAST + RANK // 2
+INVERSES = SQUARES
+NORMS = INVERSES + (FOUR + 1) * (RANK // 2)
+FACTOR_ROWS = NORMS + 8
+
+
+def fold(x):
+    return jnp.concatenate([x[: RANK // 2], x[RANK // 2 :]], axis=1)
+
+
+def unfold(x):
+    return jnp.concatenate([x[:, :RANK], x[:, RANK:]], axis=0)
+
+
+def square_iota():
+    row = lax.broadcasted_iota(jnp.int32, (RANK, RANK), 0)
+    lane = lax.broadcasted_iota(jnp.int32, (RANK, RANK), 1)
+    return row, lane
+
+
+def products_kernel(h_ref, b_ref, p_ref, o_ref):
     mats, rows, _ = b_ref.shape
     half = rows // 2
-    rank = 64
-    step = rank + rank // 2
-    for s in range(slots):
-        i = jnp.minimum(h_ref[0] * slots + s, mats - 1)
+    h = h_ref[0]
+    row, lane = square_iota()
+    grams = []
+    for s in range(FOUR + 1):
+        i = mats - 1 if s == FOUR else h * FOUR + s
         b = b_ref[i]
-        pp = p_ref[pl.ds(pl.multiple_of(i * half, 8), half), :]
+        at = i * half if s == FOUR else pl.multiple_of(i * half, 8)
+        pp = p_ref[pl.ds(at, half), :]
         full = dot(pp, jnp.concatenate([b[:half], b[half:], pp], axis=1), 0, 0)
-        gram = full[:rank, 256 : 256 + rank] + full[rank:, 256 + rank :]
-        o_ref[pl.ds(s * step, rank), :] = full[:rank, :128] + full[rank:, 128:256]
-        o_ref[pl.ds(s * step + rank, rank // 2), :] = jnp.concatenate(
-            [gram[: rank // 2], gram[rank // 2 :]], axis=1
-        )
-
-
-def factor_kernel(gy_ref, o_ref, a_ref, h_ref, *, slots):
-    rank = 64
+        y = full[:RANK, :128] + full[RANK:, 128:256]
+        if s == FOUR:
+            o_ref[pl.ds(SHARED, RANK // 2), :] = fold(jnp.where(h == 0, y[:, :RANK], y[:, RANK:]))
+        else:
+            o_ref[pl.ds(s * RANK, RANK), :] = y
+        grams.append(full[:RANK, 256 : 256 + RANK] + full[RANK:, 256 + RANK :])
+    quarter = RANK // 2
+    row32 = lax.broadcasted_iota(jnp.int32, (quarter, quarter), 0)
+    extra = jnp.zeros((quarter, quarter), F32)
+    for t in range(2):
+        lower, upper = grams[2 * t], grams[2 * t + 1]
+        o_ref[pl.ds(SQUARES + t * quarter, quarter), :] = fold(jnp.where(lane <= row, lower, upper))
+        diag = jnp.sum(jnp.where(lane == row, upper, 0.0), axis=0, keepdims=True)
+        extra = jnp.where(row32 == 2 * t, diag[:, :quarter], extra)
+        extra = jnp.where(row32 == 2 * t + 1, diag[:, quarter:], extra)
+    last = grams[FOUR]
+    o_ref[pl.ds(LAST, quarter), :] = jnp.concatenate(
+        [last[:quarter, :quarter], last[quarter:], extra], axis=1
+    )
+
+
+def read_grams(gy_ref):
+    quarter = RANK // 2
+    row, lane = square_iota()
+    last = gy_ref[pl.ds(LAST, quarter), :]
+    extra = last[:, 3 * quarter :]
+    grams = []
+    for t in range(2):
+        square = unfold(gy_ref[pl.ds(SQUARES + t * quarter, quarter), :])
+        other = jnp.transpose(square)
+        diag = jnp.concatenate([extra[2 * t : 2 * t + 1], extra[2 * t + 1 : 2 * t + 2]], axis=1)
+        grams.append(jnp.where(lane <= row, square, other))
+        grams.append(jnp.where(lane == row, diag, jnp.where(lane > row, square, other)))
+    bottom = last[:, quarter : 3 * quarter]
+    top = jnp.concatenate([last[:, :quarter], jnp.transpose(bottom[:, :quarter])], axis=1)
+    grams.append(jnp.concatenate([top, bottom], axis=0))
+    return grams
+
+
+def factor_kernel(gy_ref, o_ref, a_ref, h_ref):
+    rank = RANK
+    slots = FOUR + 1
     size = 16
-    step = rank + rank // 2
-    row = lax.broadcasted_iota(jnp.int32, (rank, rank), 0)
-    lane = lax.broadcasted_iota(jnp.int32, (rank, rank), 1)
+    row, lane = square_iota()
     eye = jnp.where(lane == row, 1.0, 0.0).astype(F32)
-    for s in range(slots):
-        packed = gy_ref[pl.ds(s * step + rank, rank // 2), :]
-        gram = jnp.concatenate([packed[:, :rank], packed[:, rank:]], axis=0)
+    for s, gram in enumerate(read_grams(gy_ref)):
         a_ref[pl.ds(s * rank, rank), :] = jnp.concatenate([gram, eye], axis=1)
     for first in range(0, rank, size):
         a = [a_ref[pl.ds(first + p, slots, stride=rank), :] for p in range(size)]
@@ -114,30 +170,49 @@
     zero = jnp.zeros((8, rank), F32)
     for s in range(slots):
         inv = h_ref[pl.ds(s * rank, rank), :][:, rank:]
-        xt = dot(inv, gy_ref[pl.ds(s * step, rank), :])
-        squares = dot(jnp.ones((8, 128), F32), xt * xt, 1, 1)
+        if s == FOUR:
+            xt = dot(inv, unfold(gy_ref[pl.ds(SHARED, rank // 2), :]))
+            o_ref[pl.ds(SHARED, rank // 2), :] = fold(xt)
+        else:
+            xt = dot(inv, gy_ref[pl.ds(s * rank, rank), :])
+            o_ref[pl.ds(s * rank, rank), :] = xt
+        squares = dot(jnp.ones((8, xt.shape[1]), F32), xt * xt, 1, 1)
         table = jnp.where(row8 == s, jnp.concatenate([squares, zero], axis=1), table)
-        o_ref[pl.ds(s * step, rank), :] = xt
-        o_ref[pl.ds(s * step + rank, rank // 2), :] = jnp.concatenate(
-            [inv[: rank // 2], inv[rank // 2 :]], axis=1
-        )
-    o_ref[pl.ds(slots * step, 8), :] = table
-
-
-def retain_kernel(core_ref, mine_ref, theirs_ref, b_ref, p_ref, mo_ref, q_ref, *, slots):
+        o_ref[pl.ds(INVERSES + s * (rank // 2), rank // 2), :] = fold(inv)
+    o_ref[pl.ds(NORMS, 8), :] = table
+
+
+def repeat_norms_kernel(mine_ref, theirs_ref, o_ref):
+    both = jnp.concatenate([mine_ref[pl.ds(NORMS, 8), :], theirs_ref[pl.ds(NORMS, 8), :]], axis=0)
+    for c in range(o_ref.shape[0]):
+        o_ref[c] = both
+
+
+def read_crossed(core, i, mine_ref, theirs_ref):
+    h, s = divmod(i, FOUR)
+    if h < 2:
+        at = pl.ds(s * RANK, RANK)
+        return jnp.where(core == h, mine_ref[at, :], theirs_ref[at, :])
+    at = pl.ds(SHARED, RANK // 2)
+    mine, theirs = unfold(mine_ref[at, :]), unfold(theirs_ref[at, :])
+    return jnp.concatenate(
+        [jnp.where(core == 0, mine, theirs), jnp.where(core == 0, theirs, mine)], axis=1
+    )
+
+
+def retain_kernel(core_ref, mine_ref, theirs_ref, b_ref, p_ref, mo_ref, q_ref):
     mats, rows, _ = b_ref.shape
     half = rows // 2
-    rank = 64
-    step = rank + rank // 2
     core = core_ref[0]
     for i in range(mats):
-        h, s = divmod(i, slots)
-        at = pl.ds(s * step, step)
-        factor = jnp.where(core == h, mine_ref[at, :], theirs_ref[at, :])
-        xt, packed = factor[:rank], factor[rank:]
-        inv = jnp.concatenate([packed[:, :rank], packed[:, rank:]], axis=0)
-        pp = p_ref[pl.ds(i * half, half), :]
-        p = jnp.concatenate([pp[:, :rank], pp[:, rank:]], axis=0)
+        h, s = divmod(i, FOUR)
+        xt = read_crossed(core, i, mine_ref, theirs_ref)
+        if h < 2:
+            at = pl.ds(INVERSES + s * (RANK // 2), RANK // 2)
+            inv = unfold(jnp.where(core == h, mine_ref[at, :], theirs_ref[at, :]))
+        else:
+            inv = unfold(mine_ref[pl.ds(INVERSES + FOUR * (RANK // 2), RANK // 2), :])
+        p = unfold(p_ref[pl.ds(i * half, half), :])
         qh, ql = parts(dot(p, inv, 1, 1, 4), 2)
         q = jnp.concatenate([qh, qh, ql, ql], axis=1)
         q_ref[i] = q
@@ -148,22 +223,24 @@
         mo_ref[i] = b_ref[i] - DECAY * low_rank
 
 
-def update_kernel(
-    core_ref, n_ref, mine_ref, theirs_ref, q_ref, u_ref, r_ref, *, slots, scale
-):
+def update_kernel(core_ref, n_ref, mine_ref, theirs_ref, q_ref, u_ref, r_ref, *, scale):
     mats = q_ref.shape[0]
-    rank = 64
-    step = rank + rank // 2
     core = core_ref[0]
     total = n_ref[0]
     for i in range(1, n_ref.shape[0]):
         total = total + n_ref[i]
+    row = lax.broadcasted_iota(jnp.int32, total.shape, 0)
+    shared = total[FOUR : FOUR + 1] + total[8 + FOUR : 9 + FOUR]
+    total = jnp.where(row == FOUR, shared, total)
     inverse = 1.0 / (jnp.sqrt(jnp.transpose(total)) + EPS)
     for i in range(mats):
-        h, s = divmod(i, slots)
-        at = pl.ds(s * step, rank)
-        xt = jnp.where(core == h, mine_ref[at, :], theirs_ref[at, :])
-        rt = xt * jnp.where(core == h, inverse[:rank, s : s + 1], inverse[:rank, 8 + s : 9 + s])
+        h, s = divmod(i, FOUR)
+        xt = read_crossed(core, i, mine_ref, theirs_ref)
+        if h < 2:
+            norm = jnp.where(core == h, inverse[:RANK, s : s + 1], inverse[:RANK, 8 + s : 9 + s])
+        else:
+            norm = inverse[:RANK, FOUR : FOUR + 1]
+        rt = xt * norm
         r_ref[i] = rt
         rh, rl = parts(scale * rt, 2)
         u_ref[i] = jnp.dot(
@@ -200,8 +277,6 @@
     far = [[(4 * h + l) * 2 + c for h in range(4)] for l in range(4) for c in range(2)]
     swap = [(i, i ^ 1) for i in range(n_row)]
     scale = math.sqrt(rows * n_row * cols * n_col / rank)
-    slots = 5
-    step = rank + rank // 2
     work = dict(flops=5 * 10**8, moved=2 * 10**6)
 
     blended = momentum + grad.astype(F32)
@@ -214,8 +289,8 @@
 
     def products(half):
         return call(
-            functools.partial(products_kernel, slots=slots),
-            shape(slots * step, 128),
+            products_kernel,
+            shape(HALF_ROWS, 128),
             half,
             blended,
             projected,
@@ -225,8 +300,8 @@
 
     theirs = lax.ppermute(products(1 - here), "row", swap)
     mine = products(here)
-    pieces = call(pair_sum_kernel, shape(slots * step, 128), mine, theirs)
-    quarter = slots * step // 4
+    pieces = call(pair_sum_kernel, shape(HALF_ROWS, 128), mine, theirs)
+    quarter = HALF_ROWS // 4
     pieces = lax.all_to_all(
         pieces.reshape(4, quarter, 128), "row", 0, 0, axis_index_groups=near
     )
@@ -236,18 +311,16 @@
     reduced = lax.all_to_all(summed, "row", 0, 0, axis_index_groups=near)
 
     mine = call(
-        functools.partial(factor_kernel, slots=slots),
-        shape(slots * step + 8, 128),
-        reduced.reshape(slots * step, 128),
-        scratch=(pltpu.VMEM((slots * rank, 128), F32),) * 2,
+        factor_kernel,
+        shape(FACTOR_ROWS, 128),
+        reduced.reshape(HALF_ROWS, 128),
+        scratch=(pltpu.VMEM(((FOUR + 1) * rank, 128), F32),) * 2,
     )
     theirs = lax.ppermute(mine, "row", swap)
-    squares = jnp.concatenate([mine[slots * step :], theirs[slots * step :]], axis=0)
-    squares = lax.all_to_all(
-        jnp.broadcast_to(squares[None], (n_col, 16, 128)), "col", 0, 0
-    )
+    squares = call(repeat_norms_kernel, shape(n_col, 16, 128), mine, theirs)
+    squares = lax.all_to_all(squares, "col", 0, 0)
     momentum_next, orthonormal = call(
-        functools.partial(retain_kernel, slots=slots),
+        retain_kernel,
         (shape(mats, rows, cols), shape(mats, rows, 4 * rank, dtype=BF16)),
         here,
         mine,
@@ -258,7 +331,7 @@
         **work,
     )
     update, right = call(
-        functools.partial(update_kernel, slots=slots, scale=scale),
+        functools.partial(update_kernel, scale=scale),
         (shape(mats, rows, cols, dtype=BF16), shape(mats, rank, cols)),
         here,
         squares,

time: 115 us -> 114 us (level)
  blocking collectives: 66.8 us -> 64.8 us
    pallas_call x10 -> x11, Pallas kernels: 10.3 us -> 11.2 us  [call(): pl.pallas_call(kernel, out_shape=out, in_specs=(first,) + (vmem,) * (len(...]
where the time goes in v4:
time: 114 us; the launch traced here: 113 us
  blocking collectives  64.8 us (57%)
  starting transfers between devices  20.3 us (18%)
  waiting for transfers between devices  14.5 us (13%)
  Pallas kernels  11.2 us (10%)
  other arithmetic  1.48 us (1%)
    all_to_all x1, blocking collectives, on_device(): pieces = lax.all_to_all(summed, 'row', 0, 0, axis_index_groups=far)  26.5 us
    all_to_all x1, blocking collectives, on_device(): pieces = lax.all_to_all(part.reshape(n_col, 64, 128), 'col', 0, 0)  16.6 us
    all_to_all x1, blocking collectives, on_device(): lax.all_to_all(pieces.reshape(4, quarter, 128), 'row', 0, 0, axis_index_g...  11.7 us
    pallas_call x11, Pallas kernels, call(): pl.pallas_call(kernel, out_shape=out, in_specs=(first,) + (vmem,) * (len(...  11.2 us
    all_to_all x1, blocking collectives, on_device(): reduced = lax.all_to_all(summed, 'row', 0, 0, axis_index_groups=near)  10 us
    all_to_all x1, waiting for transfers between devices, on_device(): projected = lax.all_to_all(summed, 'col', 0, 0).reshape(1024, 128)  8.91 us
    ppermute x1, starting transfers between devices, on_device(): theirs = lax.ppermute(mine, 'row', swap)  6.94 us
    ppermute x1, starting transfers between devices, on_device(): theirs = lax.ppermute(products(1 - here), 'row', swap)  6.28 us
  transfers between devices with their start and end apart: 4, of which 4 were waited for; matrix products, arithmetic and copies ran while one was open for 0% of the time, Pallas kernels for 3%

profile of v4, /device:TPU:1, one launch (start us, length us, event | category | flops | bytes accessed | tf_op | source)
XLA Modules:
  0.0 113.0 jit_solution(1935977333019987280)
XLA Ops:
  0.6 0.0 copy-start
  0.6 1.5 %convert_add_fusion.b_ref = f32[9,224,128]{2,1,0:T(8,128)S(1)} fusion(f32[9,224,128]{2,1,0:T(8,128)} %param.4, bf16[9,224,128]{2,1,0:T(8,128)(2,1)} %param.3), kind=kLoop, calls=%fused_computation | loop fusion | flops 516096 | bytes 2580480 | tf_op jit(solution)/shard_map/add | solution.py:282
  2.1 0.0 copy-done
  2.1 0.6 shard_map.58
  2.8 16.6 %all_to_all.30.x_ref = f32[16,64,128]{2,1,0:T(8,128)S(1)} all-to-all(f32[16,64,128]{2,1,0:T(8,128)S(1)} %bitcast.10), channel_id=1, replica_groups=mesh['row'=32,'col'=16] {'col'}, dimensions={0} | all-to-all | bytes 1048576 | tf_op jit(solution)/shard_map/all_to_all | solution.py:286
  19.4 0.9 shard_map.59
  20.2 3.6 %all-to-all-start.1 = ((f32[16,64,128]{2,1,0:T(8,128)}), f32[16,64,128]{2,1,0:T(8,128)S(1)}, u32[]{:S(2)}, u32[]{:S(2)}) async-start(f32[16,64,128]{2,1,0:T(8,128)} %shard_map.59), calls=%async_computation.1 | async-start | bytes 1048576 | tf_op jit(solution)/shard_map/all_to_all | solution.py:288
  23.8 8.9 %all-to-all-done.1 = f32[16,64,128]{2,1,0:T(8,128)S(1)} async-done(((f32[16,64,128]{2,1,0:T(8,128)}), f32[16,64,128]{2,1,0:T(8,128)S(1)}, u32[]{:S(2)}, u32[]{:S(2)}) %all-to-all-start.1) | async-done | bytes 524320 | tf_op jit(solution)/shard_map/all_to_all | solution.py:288
  32.7 0.9 shard_map.61
  33.6 6.3 %collective-permute-start = (f32[384,128]{1,0:T(8,128)S(1)}, f32[384,128]{1,0:T(8,128)S(1)}, u32[]{:S(2)}, u32[]{:S(2)}) collective-permute-start(f32[384,128]{1,0:T(8,128)S(1)} %shard_map.61), channel_id=1, source_target_pairs={{0,16},{16,0},{32,48},{48,32},{64,80},{80,64},{96,112},{112,96},{1... | collective-permute-start | bytes 589832 | tf_op jit(solution)/shard_map/ppermute | solution.py:301
  39.9 0.9 shard_map.60.x_ref
  40.8 0.2 collective-permute-done.y_ref
  41.0 11.7 %all_to_all.31.x_ref = f32[4,96,128]{2,1,0:T(8,128)S(1)} all-to-all(f32[4,96,128]{2,1,0:T(8,128)S(1)} %bitcast.11), channel_id=1, replica_groups={{0,32,64,96},{16,48,80,112},{128,160,192,224},{144,176,208,240},{256,28..., dimensions={0} | all-to-all | bytes 393216 | tf_op jit(solution)/shard_map/all_to_all | solution.py:305
  52.6 26.5 %all_to_all.32.x_ref = f32[4,96,128]{2,1,0:T(8,128)S(1)} all-to-all(f32[4,96,128]{2,1,0:T(8,128)S(1)} %shard_map.63), channel_id=1, replica_groups={{0,128,256,384},{16,144,272,400},{32,160,288,416},{48,176,304,432},{64,..., dimensions={0} | all-to-all | bytes 393216 | tf_op jit(solution)/shard_map/all_to_all | solution.py:309
  79.2 10.0 %all_to_all.33 = f32[4,96,128]{2,1,0:T(8,128)S(1)} all-to-all(f32[4,96,128]{2,1,0:T(8,128)S(1)} %shard_map.64), channel_id=1, replica_groups={{0,32,64,96},{16,48,80,112},{128,160,192,224},{144,176,208,240},{256,28..., dimensions={0} | all-to-all | bytes 393216 | tf_op jit(solution)/shard_map/all_to_all | solution.py:311
  89.2 3.4 %shard_map.65.mine_ref = f32[456,128]{1,0:T(8,128)S(1)} custom-call(f32[384,128]{1,0:T(8,128)S(1)} %bitcast.12), custom_call_target="tpu_custom_call" | custom-call | tf_op jit(solution)/shard_map/pallas_call | solution.py:254
  92.6 6.9 %collective-permute-start.1 = (f32[456,128]{1,0:T(8,128)S(1)}, f32[456,128]{1,0:T(8,128)S(1)}, u32[]{:S(2)}, u32[]{:S(2)}) collective-permute-start(f32[456,128]{1,0:T(8,128)S(1)} %shard_map.65.mine_ref), channel_id=1, source_target_pairs={{0,16},{16,0},{32,48},{48,32},{64,80},{80,64},{96,112},{112,96},{1... | collective-permute-start | bytes 700424 | tf_op jit(solution)/shard_map/ppermute | solution.py:319
  99.6 1.1 collective-permute-done.1.theirs_ref
  100.7 0.7 shard_map.66
  101.3 3.5 %all-to-all-start.5 = ((f32[16,16,128]{2,1,0:T(8,128)}), f32[16,16,128]{2,1,0:T(8,128)S(1)}, u32[]{:S(2)}, u32[]{:S(2)}) async-start(f32[16,16,128]{2,1,0:T(8,128)} %shard_map.66), calls=%async_computation.5 | async-start | bytes 262144 | tf_op jit(solution)/shard_map/all_to_all | solution.py:321
  104.9 2.4 %shard_map.67 = (f32[9,224,128]{2,1,0:T(8,128)}, bf16[9,224,256]{2,1,0:T(8,128)(2,1)S(1)}) custom-call(s32[1]{0:T(128)} %bitcast.h_ref.core_ref, f32[456,128]{1,0:T(8,128)S(1)} %shard_map.65.mine_ref, f32[456,128]{1,0:T(8,128)S(1)} %collective-permute-done.1.theirs_ref, f32[9,224,128]{2,1,0:T(8,128)S(1)} %convert_add_fusion.b_ref, f32[1024,128]{1,0:T(8,128)S(1)} %bitcast.9), custom_call_target="tpu_custom_call" | custom-call | flops 500000000 | bytes 2000000 | tf_op jit(solution)/shard_map/pallas_call | solution.py:254
  107.2 4.4 %all-to-all-done.5.n_ref = f32[16,16,128]{2,1,0:T(8,128)S(1)} async-done(((f32[16,16,128]{2,1,0:T(8,128)}), f32[16,16,128]{2,1,0:T(8,128)S(1)}, u32[]{:S(2)}, u32[]{:S(2)}) %all-to-all-start.5) | async-done | bytes 131104 | tf_op jit(solution)/shard_map/all_to_all | solution.py:321
  111.6 1.5 %shard_map.68 = (bf16[9,224,128]{2,1,0:T(8,128)(2,1)}, f32[9,64,128]{2,1,0:T(8,128)}) custom-call(s32[1]{0:T(128)} %bitcast.h_ref.core_ref, f32[16,16,128]{2,1,0:T(8,128)S(1)} %all-to-all-done.5.n_ref, f32[456,128]{1,0:T(8,128)S(1)} %shard_map.65.mine_ref, f32[456,128]{1,0:T(8,128)S(1)} %collective-permute-done.1.theirs_ref, ...), custom_call_target="tpu_custom_call" | custom-call | tf_op jit(solution)/shard_map/pallas_call | solution.py:254
  (3 shorter events, 0.1 us)
Async XLA Ops:
  0.6 1.5 %copy-start = (f32[9,128,64]{1,2,0:T(8,128)S(1)}, f32[9,128,64]{1,2,0:T(8,128)}, u32[]{:S(2)}) copy-start(f32[9,128,64]{1,2,0:T(8,128)} %param.5) | copy-start | bytes 884740
  20.2 12.5 %all-to-all-start.1 = ((f32[16,64,128]{2,1,0:T(8,128)}), f32[16,64,128]{2,1,0:T(8,128)S(1)}, u32[]{:S(2)}, u32[]{:S(2)}) async-start(f32[16,64,128]{2,1,0:T(8,128)} %shard_map.59), calls=%async_computation.1 | async-start | bytes 1048576 | tf_op jit(solution)/shard_map/all_to_all | solution.py:288
  33.6 7.3 %collective-permute-start = (f32[384,128]{1,0:T(8,128)S(1)}, f32[384,128]{1,0:T(8,128)S(1)}, u32[]{:S(2)}, u32[]{:S(2)}) collective-permute-start(f32[384,128]{1,0:T(8,128)S(1)} %shard_map.61), channel_id=1, source_target_pairs={{0,16},{16,0},{32,48},{48,32},{64,80},{80,64},{96,112},{112,96},{1... | collective-permute-start | bytes 589832 | tf_op jit(solution)/shard_map/ppermute | solution.py:301
  92.6 8.0 %collective-permute-start.1 = (f32[456,128]{1,0:T(8,128)S(1)}, f32[456,128]{1,0:T(8,128)S(1)}, u32[]{:S(2)}, u32[]{:S(2)}) collective-permute-start(f32[456,128]{1,0:T(8,128)S(1)} %shard_map.65.mine_ref), channel_id=1, source_target_pairs={{0,16},{16,0},{32,48},{48,32},{64,80},{80,64},{96,112},{112,96},{1... | collective-permute-start | bytes 700424 | tf_op jit(solution)/shard_map/ppermute | solution.py:319
  101.3 10.2 %all-to-all-start.5 = ((f32[16,16,128]{2,1,0:T(8,128)}), f32[16,16,128]{2,1,0:T(8,128)S(1)}, u32[]{:S(2)}, u32[]{:S(2)}) async-start(f32[16,16,128]{2,1,0:T(8,128)} %shard_map.66), calls=%async_computation.5 | async-start | bytes 262144 | tf_op jit(solution)/shard_map/all_to_all | solution.py:321

commit v5 on v4

--- a/solution.py
+++ b/solution.py
@@ -61,8 +61,7 @@
 LAST = SQUARES + 2 * (RANK // 2)
 HALF_ROWS = LAST + RANK // 2
 INVERSES = SQUARES
-NORMS = INVERSES + (FOUR + 1) * (RANK // 2)
-FACTOR_ROWS = NORMS + 8
+FACTOR_ROWS = INVERSES + (FOUR + 1) * (RANK // 2)
 
 
 def fold(x):
@@ -130,7 +129,7 @@
     return grams
 
 
-def factor_kernel(gy_ref, o_ref, a_ref, h_ref):
+def factor_kernel(gy_ref, o_ref, n_ref, a_ref, h_ref):
     rank = RANK
     slots = FOUR + 1
     size = 16
@@ -149,7 +148,6 @@
         ]
         for p in range(size):
             root = lax.rsqrt(e[p][p])
-            root = root * (1.5 - 0.5 * e[p][p] * root * root)
             a[p] = a[p] * root
             low = [None] * size
             for i in range(p + 1, size):
@@ -179,13 +177,8 @@
         squares = dot(jnp.ones((8, xt.shape[1]), F32), xt * xt, 1, 1)
         table = jnp.where(row8 == s, jnp.concatenate([squares, zero], axis=1), table)
         o_ref[pl.ds(INVERSES + s * (rank // 2), rank // 2), :] = fold(inv)
-    o_ref[pl.ds(NORMS, 8), :] = table
-
-
-def repeat_norms_kernel(mine_ref, theirs_ref, o_ref):
-    both = jnp.concatenate([mine_ref[pl.ds(NORMS, 8), :], theirs_ref[pl.ds(NORMS, 8), :]], axis=0)
-    for c in range(o_ref.shape[0]):
-        o_ref[c] = both
+    for c in range(n_ref.shape[0]):
+        n_ref[c] = table
 
 
 def read_crossed(core, i, mine_ref, theirs_ref):
@@ -226,21 +219,18 @@
 def update_kernel(core_ref, n_ref, mine_ref, theirs_ref, q_ref, u_ref, r_ref, *, scale):
     mats = q_ref.shape[0]
     core = core_ref[0]
-    total = n_ref[0]
-    for i in range(1, n_ref.shape[0]):
-        total = total + n_ref[i]
-    row = lax.broadcasted_iota(jnp.int32, total.shape, 0)
-    shared = total[FOUR : FOUR + 1] + total[8 + FOUR : 9 + FOUR]
-    total = jnp.where(row == FOUR, shared, total)
+    totals = [n_ref[0], n_ref[1]]
+    for i in range(2, n_ref.shape[0]):
+        totals[i % 2] = totals[i % 2] + n_ref[i]
+    row = lax.broadcasted_iota(jnp.int32, totals[0].shape, 0)
+    totals[0] = jnp.where(row == FOUR, totals[0] + totals[1], totals[0])
+    total = jnp.concatenate(totals, axis=0)
     inverse = 1.0 / (jnp.sqrt(jnp.transpose(total)) + EPS)
     for i in range(mats):
         h, s = divmod(i, FOUR)
         xt = read_crossed(core, i, mine_ref, theirs_ref)
-        if h < 2:
-            norm = jnp.where(core == h, inverse[:RANK, s : s + 1], inverse[:RANK, 8 + s : 9 + s])
-        else:
-            norm = inverse[:RANK, FOUR : FOUR + 1]
-        rt = xt * norm
+        at = 8 * h + s if h < 2 else FOUR
+        rt = xt * inverse[:RANK, at : at + 1]
         r_ref[i] = rt
         rh, rl = parts(scale * rt, 2)
         u_ref[i] = jnp.dot(
@@ -272,14 +262,18 @@
     n_col = lax.axis_size("col")
     n_row = lax.axis_size("row")
     core = lax.rem(lax.axis_index("row"), 2)
-    here = core.reshape(1)
-    near = [[(4 * h + l) * 2 + c for l in range(4)] for h in range(4) for c in range(2)]
+    near = [[(4 * h + l) * 2 + c for l in (1, 0, 2, 3)] for h in range(4) for c in range(2)]
+    plane = [
+        [(2 * z + c) * n_col + k for k in range(n_col) for c in range(2)] for z in range(n_row // 2)
+    ]
     far = [[(4 * h + l) * 2 + c for h in range(4)] for l in range(4) for c in range(2)]
     swap = [(i, i ^ 1) for i in range(n_row)]
     scale = math.sqrt(rows * n_row * cols * n_col / rank)
     work = dict(flops=5 * 10**8, moved=2 * 10**6)
 
-    blended = momentum + grad.astype(F32)
+    blended, here, there = lax.optimization_barrier(
+        (momentum + grad.astype(F32), core.reshape(1), 1 - core.reshape(1))
+    )
     part = call(
         project_kernel, shape(1024, 128), blended, jnp.swapaxes(trailing_coefficients, 1, 2)
     )
@@ -298,7 +292,7 @@
             **work,
         )
 
-    theirs = lax.ppermute(products(1 - here), "row", swap)
+    theirs = lax.ppermute(products(there), "row", swap)
     mine = products(here)
     pieces = call(pair_sum_kernel, shape(HALF_ROWS, 128), mine, theirs)
     quarter = HALF_ROWS // 4
@@ -310,15 +304,14 @@
     summed = call(sum_kernel, shape(4, quarter, 128), pieces)
     reduced = lax.all_to_all(summed, "row", 0, 0, axis_index_groups=near)
 
-    mine = call(
+    mine, squares = call(
         factor_kernel,
-        shape(FACTOR_ROWS, 128),
+        (shape(FACTOR_ROWS, 128), shape(2 * n_col, 8, 128)),
         reduced.reshape(HALF_ROWS, 128),
         scratch=(pltpu.VMEM(((FOUR + 1) * rank, 128), F32),) * 2,
     )
     theirs = lax.ppermute(mine, "row", swap)
-    squares = call(repeat_norms_kernel, shape(n_col, 16, 128), mine, theirs)
-    squares = lax.all_to_all(squares, "col", 0, 0)
+    squares = lax.all_to_all(squares, ("row", "col"), 0, 0, axis_index_groups=plane)
     momentum_next, orthonormal = call(
         retain_kernel,
         (shape(mats, rows, cols), shape(mats, rows, 4 * rank, dtype=BF16)),

time: 114 us -> 110 us (0.965)
  blocking collectives: 64.8 us -> 73.9 us
  waiting for transfers between devices: 14.5 us -> 5.5 us
  starting transfers between devices: 20.3 us -> 18 us
    all_to_all x0 -> x1, blocking collectives: none -> 12.1 us  [on_device(): projected = lax.all_to_all(summed, 'col', 0, 0).reshape(1024, 128)]
    all_to_all x2 -> x1, waiting for transfers between devices: 13.3 us -> 5.33 us  [on_device(): lax.all_to_all(squares, ('row', 'col'), 0, 0, axis_index_groups=plane)]
    all_to_all x2 -> x1, starting transfers between devices: 7.09 us -> 3.66 us  [on_device(): lax.all_to_all(squares, ('row', 'col'), 0, 0, axis_index_groups=plane)]
    all_to_all x1, blocking collectives: 10 us -> 7.77 us  [on_device(): reduced = lax.all_to_all(summed, 'row', 0, 0, axis_index_groups=near)]
    pallas_call x11 -> x10, Pallas kernels: 11.2 us -> 10.3 us  [call(): pl.pallas_call(kernel, out_shape=out, in_specs=(first,) + (vmem,) * (len(...]
  transfers between devices with their start and end apart: 4 -> 3, of which waited for: 4 -> 2; matrix products, arithmetic and copies ran while one was open for 0% -> 0% of each run, Pallas kernels for 3% -> 3%
where the time goes in v5:
time: 110 us
  blocking collectives  73.9 us (67%)
  starting transfers between devices  18 us (16%)
  Pallas kernels  10.3 us (9%)
  waiting for transfers between devices  5.5 us (5%)
  other arithmetic  1.48 us (1%)
    all_to_all x1, blocking collectives, on_device(): pieces = lax.all_to_all(summed, 'row', 0, 0, axis_index_groups=far)  26.2 us
    all_to_all x1, blocking collectives, on_device(): pieces = lax.all_to_all(part.reshape(n_col, 64, 128), 'col', 0, 0)  16.6 us
    all_to_all x1, blocking collectives, on_device(): projected = lax.all_to_all(summed, 'col', 0, 0).reshape(1024, 128)  12.1 us
    all_to_all x1, blocking collectives, on_device(): lax.all_to_all(pieces.reshape(4, quarter, 128), 'row', 0, 0, axis_index_g...  11.2 us
    pallas_call x10, Pallas kernels, call(): pl.pallas_call(kernel, out_shape=out, in_specs=(first,) + (vmem,) * (len(...  10.3 us
    ppermute x1, starting transfers between devices, on_device(): theirs = lax.ppermute(mine, 'row', swap)  7.97 us
    all_to_all x1, blocking collectives, on_device(): reduced = lax.all_to_all(summed, 'row', 0, 0, axis_index_groups=near)  7.77 us
    ppermute x1, starting transfers between devices, on_device(): theirs = lax.ppermute(products(there), 'row', swap)  6.37 us
  transfers between devices with their start and end apart: 3, of which 2 were waited for; matrix products, arithmetic and copies ran while one was open for 0% of the time, Pallas kernels for 3%

profile of v5, /device:TPU:1, one launch (start us, length us, event | category | flops | bytes accessed | tf_op | source)
XLA Modules:
  0.0 109.8 jit_solution(6376493225646454774)
XLA Ops:
  0.6 0.0 copy-start
  0.6 1.5 %convert_add_fusion.b_ref = f32[9,224,128]{2,1,0:T(8,128)S(1)} fusion(f32[9,224,128]{2,1,0:T(8,128)} %param.4, bf16[9,224,128]{2,1,0:T(8,128)(2,1)} %param.3), kind=kLoop, calls=%fused_computation | loop fusion | flops 516096 | bytes 2580480 | tf_op jit(solution)/shard_map/add | solution.py:275
  2.1 0.0 copy-done
  2.1 0.6 shard_map.58
  2.8 16.6 %all_to_all.30.x_ref = f32[16,64,128]{2,1,0:T(8,128)S(1)} all-to-all(f32[16,64,128]{2,1,0:T(8,128)S(1)} %bitcast.10), channel_id=1, replica_groups=mesh['row'=32,'col'=16] {'col'}, dimensions={0} | all-to-all | bytes 1048576 | tf_op jit(solution)/shard_map/all_to_all | solution.py:280
  19.4 0.1 shard_map.59
  19.4 12.1 %all_to_all.31 = f32[16,64,128]{2,1,0:T(8,128)S(1)} all-to-all(f32[16,64,128]{2,1,0:T(8,128)S(1)} %shard_map.59), channel_id=1, replica_groups=mesh['row'=32,'col'=16] {'col'}, dimensions={0} | all-to-all | bytes 1048576 | tf_op jit(solution)/shard_map/all_to_all | solution.py:282
  31.5 0.9 shard_map.61
  32.4 6.4 %collective-permute-start = (f32[384,128]{1,0:T(8,128)S(1)}, f32[384,128]{1,0:T(8,128)S(1)}, u32[]{:S(2)}, u32[]{:S(2)}) collective-permute-start(f32[384,128]{1,0:T(8,128)S(1)} %shard_map.61), channel_id=1, source_target_pairs={{0,16},{16,0},{32,48},{48,32},{64,80},{80,64},{96,112},{112,96},{1... | collective-permute-start | bytes 589832 | tf_op jit(solution)/shard_map/ppermute | solution.py:295
  38.8 0.9 shard_map.60.x_ref
  39.7 0.2 collective-permute-done.y_ref
  39.9 11.2 %all_to_all.32.x_ref = f32[4,96,128]{2,1,0:T(8,128)S(1)} all-to-all(f32[4,96,128]{2,1,0:T(8,128)S(1)} %bitcast.12), channel_id=1, replica_groups={{32,0,64,96},{48,16,80,112},{160,128,192,224},{176,144,208,240},{288,25..., dimensions={0} | all-to-all | bytes 393216 | tf_op jit(solution)/shard_map/all_to_all | solution.py:299
  51.1 26.2 %all_to_all.33.x_ref = f32[4,96,128]{2,1,0:T(8,128)S(1)} all-to-all(f32[4,96,128]{2,1,0:T(8,128)S(1)} %shard_map.63), channel_id=1, replica_groups={{0,128,256,384},{16,144,272,400},{32,160,288,416},{48,176,304,432},{64,..., dimensions={0} | all-to-all | bytes 393216 | tf_op jit(solution)/shard_map/all_to_all | solution.py:303
  77.3 7.8 %all_to_all.34 = f32[4,96,128]{2,1,0:T(8,128)S(1)} all-to-all(f32[4,96,128]{2,1,0:T(8,128)S(1)} %shard_map.64), channel_id=1, replica_groups={{32,0,64,96},{48,16,80,112},{160,128,192,224},{176,144,208,240},{288,25..., dimensions={0} | all-to-all | bytes 393216 | tf_op jit(solution)/shard_map/all_to_all | solution.py:305
  85.1 4.0 %shard_map.65 = (f32[448,128]{1,0:T(8,128)S(1)}, f32[32,8,128]{2,1,0:T(8,128)}) custom-call(f32[384,128]{1,0:T(8,128)S(1)} %bitcast.11), custom_call_target="tpu_custom_call" | custom-call | tf_op jit(solution)/shard_map/pallas_call | solution.py:244
  89.1 8.0 %collective-permute-start.1 = (f32[448,128]{1,0:T(8,128)S(1)}, f32[448,128]{1,0:T(8,128)S(1)}, u32[]{:S(2)}, u32[]{:S(2)}) collective-permute-start(f32[448,128]{1,0:T(8,128)S(1)} %get-tuple-element.16.mine_ref), channel_id=1, source_target_pairs={{0,16},{16,0},{32,48},{48,32},{64,80},{80,64},{96,112},{112,96},{1... | collective-permute-start | bytes 688136 | tf_op jit(solution)/shard_map/ppermute | solution.py:313
  97.1 3.7 %all-to-all-start.5 = ((f32[32,8,128]{2,1,0:T(8,128)}), f32[32,8,128]{2,1,0:T(8,128)S(1)}, u32[]{:S(2)}, u32[]{:S(2)}) async-start(f32[32,8,128]{2,1,0:T(8,128)} %get-tuple-element.15), calls=%async_computation.5 | async-start | bytes 262144 | tf_op jit(solution)/shard_map/all_to_all | solution.py:314
  100.7 0.0 collective-permute-done.1.theirs_ref
  100.7 2.4 %shard_map.66 = (f32[9,224,128]{2,1,0:T(8,128)}, bf16[9,224,256]{2,1,0:T(8,128)(2,1)S(1)}) custom-call(s32[1]{0:T(128)} %bitcast.h_ref.core_ref, f32[448,128]{1,0:T(8,128)S(1)} %get-tuple-element.16.mine_ref, f32[448,128]{1,0:T(8,128)S(1)} %collective-permute-done.1.theirs_ref, f32[9,224,128]{2,1,0:T(8,128)S(1)} %convert_add_fusion.b_ref, ...), custom_call_target="tpu_custom_call" | custom-call | flops 500000000 | bytes 2000000 | tf_op jit(solution)/shard_map/pallas_call | solution.py:244
  103.1 5.3 %all-to-all-done.5.n_ref = f32[32,8,128]{2,1,0:T(8,128)S(1)} async-done(((f32[32,8,128]{2,1,0:T(8,128)}), f32[32,8,128]{2,1,0:T(8,128)S(1)}, u32[]{:S(2)}, u32[]{:S(2)}) %all-to-all-start.5) | async-done | bytes 131104 | tf_op jit(solution)/shard_map/all_to_all | solution.py:314
  108.4 1.4 %shard_map.67 = (bf16[9,224,128]{2,1,0:T(8,128)(2,1)}, f32[9,64,128]{2,1,0:T(8,128)}) custom-call(s32[1]{0:T(128)} %bitcast.h_ref.core_ref, f32[32,8,128]{2,1,0:T(8,128)S(1)} %all-to-all-done.5.n_ref, f32[448,128]{1,0:T(8,128)S(1)} %get-tuple-element.16.mine_ref, f32[448,128]{1,0:T(8,128)S(1)} %collective-permute-done.1.theirs_ref, ...), custom_call_target="tpu_custom_call" | custom-call | tf_op jit(solution)/shard_map/pallas_call | solution.py:244
  (3 shorter events, 0.1 us)
Async XLA Ops:
  0.6 1.5 %copy-start = (f32[9,128,64]{1,2,0:T(8,128)S(1)}, f32[9,128,64]{1,2,0:T(8,128)}, u32[]{:S(2)}) copy-start(f32[9,128,64]{1,2,0:T(8,128)} %param.5) | copy-start | bytes 884740
  32.4 7.4 %collective-permute-start = (f32[384,128]{1,0:T(8,128)S(1)}, f32[384,128]{1,0:T(8,128)S(1)}, u32[]{:S(2)}, u32[]{:S(2)}) collective-permute-start(f32[384,128]{1,0:T(8,128)S(1)} %shard_map.61), channel_id=1, source_target_pairs={{0,16},{16,0},{32,48},{48,32},{64,80},{80,64},{96,112},{112,96},{1... | collective-permute-start | bytes 589832 | tf_op jit(solution)/shard_map/ppermute | solution.py:295
  89.1 11.6 %collective-permute-start.1 = (f32[448,128]{1,0:T(8,128)S(1)}, f32[448,128]{1,0:T(8,128)S(1)}, u32[]{:S(2)}, u32[]{:S(2)}) collective-permute-start(f32[448,128]{1,0:T(8,128)S(1)} %get-tuple-element.16.mine_ref), channel_id=1, source_target_pairs={{0,16},{16,0},{32,48},{48,32},{64,80},{80,64},{96,112},{112,96},{1... | collective-permute-start | bytes 688136 | tf_op jit(solution)/shard_map/ppermute | solution.py:313
  97.1 11.4 %all-to-all-start.5 = ((f32[32,8,128]{2,1,0:T(8,128)}), f32[32,8,128]{2,1,0:T(8,128)S(1)}, u32[]{:S(2)}, u32[]{:S(2)}) async-start(f32[32,8,128]{2,1,0:T(8,128)} %get-tuple-element.15), calls=%async_computation.5 | async-start | bytes 262144 | tf_op jit(solution)/shard_map/all_to_all | solution.py:314

commit v6 on v5

--- a/solution.py
+++ b/solution.py
@@ -12,6 +12,9 @@
 EPS = 1e-08
 F32 = jnp.float32
 BF16 = jnp.bfloat16
+HUB = 10
+NEAR = (2, 1, 3, 0)
+FAR = (2, 0, 1, 3)
 ORDER = ((0, 0), (0, 1), (1, 0), (1, 1), (0, 2), (2, 0))
 
 
@@ -262,11 +265,10 @@
     n_col = lax.axis_size("col")
     n_row = lax.axis_size("row")
     core = lax.rem(lax.axis_index("row"), 2)
-    near = [[(4 * h + l) * 2 + c for l in (1, 0, 2, 3)] for h in range(4) for c in range(2)]
-    plane = [
-        [(2 * z + c) * n_col + k for k in range(n_col) for c in range(2)] for z in range(n_row // 2)
-    ]
-    far = [[(4 * h + l) * 2 + c for h in range(4)] for l in range(4) for c in range(2)]
+    near = [[(4 * h + l) * 2 + c for l in NEAR] for h in range(4) for c in range(2)]
+    order = [HUB, *(k for k in range(n_col) if k != HUB)]
+    plane = [[(2 * z + c) * n_col + k for k in order for c in range(2)] for z in range(n_row // 2)]
+    far = [[(4 * h + l) * 2 + c for h in FAR] for l in range(4) for c in range(2)]
     swap = [(i, i ^ 1) for i in range(n_row)]
     scale = math.sqrt(rows * n_row * cols * n_col / rank)
     work = dict(flops=5 * 10**8, moved=2 * 10**6)
@@ -277,9 +279,12 @@
     part = call(
         project_kernel, shape(1024, 128), blended, jnp.swapaxes(trailing_coefficients, 1, 2)
     )
-    pieces = lax.all_to_all(part.reshape(n_col, 64, 128), "col", 0, 0)
+    pieces = lax.all_to_all(
+        part.reshape(n_col, 64, 128), "col", 0, 0, axis_index_groups=[order]
+    )
     summed = call(sum_kernel, shape(n_col, 64, 128), pieces)
-    projected = lax.all_to_all(summed, "col", 0, 0).reshape(1024, 128)
+    projected = lax.all_to_all(summed, "col", 0, 0, axis_index_groups=[order])
+    projected = projected.reshape(1024, 128)
 
     def products(half):
         return call(

time: 110 us -> 99 us (0.900)
  blocking collectives: 73.9 us -> 63.3 us
  waiting for transfers between devices: 5.5 us -> 0.63 us
  starting transfers between devices: 18 us -> 22.2 us
    all_to_all x1, waiting for transfers between devices: 5.33 us -> 0.46 us  [on_device(): lax.all_to_all(squares, ('row', 'col'), 0, 0, axis_index_groups=plane)]
    all_to_all x1, starting transfers between devices: 3.66 us -> 8.46 us  [on_device(): lax.all_to_all(squares, ('row', 'col'), 0, 0, axis_index_groups=plane)]
    all_to_all x1, blocking collectives: 26.2 us -> 21.9 us  [on_device(): pieces = lax.all_to_all(summed, 'row', 0, 0, axis_index_groups=far)]
    all_to_all x1, blocking collectives: 11.2 us -> 7.5 us  [on_device(): lax.all_to_all(pieces.reshape(4, quarter, 128), 'row', 0, 0, axis_index_g...]
    all_to_all x2, blocking collectives: 28.7 us -> 25.3 us  [the longest x1 13.2 us: on_device(): lax.all_to_all(part.reshape(n_col, 64, 128), 'col', 0, 0, axis_index_grou...]
    ppermute x1, starting transfers between devices: 7.97 us -> 5.13 us  [on_device(): theirs = lax.ppermute(mine, 'row', swap)]
    ppermute x1, starting transfers between devices: 6.37 us -> 8.6 us  [on_device(): theirs = lax.ppermute(products(there), 'row', swap)]
where the time goes in v6:
time: 99 us; the launch traced here: 98.6 us
  blocking collectives  63.3 us (64%)
  starting transfers between devices  22.2 us (22%)
  Pallas kernels  10.3 us (10%)
  other arithmetic  1.48 us (1%)
    all_to_all x1, blocking collectives, on_device(): pieces = lax.all_to_all(summed, 'row', 0, 0, axis_index_groups=far)  21.9 us
    all_to_all x1, blocking collectives, on_device(): lax.all_to_all(part.reshape(n_col, 64, 128), 'col', 0, 0, axis_index_grou...  13.2 us
    all_to_all x1, blocking collectives, on_device(): projected = lax.all_to_all(summed, 'col', 0, 0, axis_index_groups=[order])  12.2 us
    pallas_call x10, Pallas kernels, call(): pl.pallas_call(kernel, out_shape=out, in_specs=(first,) + (vmem,) * (len(...  10.3 us
    ppermute x1, starting transfers between devices, on_device(): theirs = lax.ppermute(products(there), 'row', swap)  8.6 us
    all_to_all x1, blocking collectives, on_device(): reduced = lax.all_to_all(summed, 'row', 0, 0, axis_index_groups=near)  8.56 us
    all_to_all x1, starting transfers between devices, on_device(): lax.all_to_all(squares, ('row', 'col'), 0, 0, axis_index_groups=plane)  8.46 us
    all_to_all x1, blocking collectives, on_device(): lax.all_to_all(pieces.reshape(4, quarter, 128), 'row', 0, 0, axis_index_g...  7.5 us
  transfers between devices with their start and end apart: 3, of which 2 were waited for; matrix products, arithmetic and copies ran while one was open for 0% of the time, Pallas kernels for 3%

profile of v6, /device:TPU:1, one launch (start us, length us, event | category | flops | bytes accessed | tf_op | source)
XLA Modules:
  0.0 98.6 jit_solution(6645617410013477746)
XLA Ops:
  0.6 0.0 copy-start
  0.6 1.5 %convert_add_fusion.b_ref = f32[9,224,128]{2,1,0:T(8,128)S(1)} fusion(f32[9,224,128]{2,1,0:T(8,128)} %param.4, bf16[9,224,128]{2,1,0:T(8,128)(2,1)} %param.3), kind=kLoop, calls=%fused_computation | loop fusion | flops 516096 | bytes 2580480 | tf_op jit(solution)/shard_map/add | solution.py:277
  2.1 0.0 copy-done
  2.1 0.6 shard_map.58
  2.8 13.2 %all_to_all.30.x_ref = f32[16,64,128]{2,1,0:T(8,128)S(1)} all-to-all(f32[16,64,128]{2,1,0:T(8,128)S(1)} %bitcast.10), channel_id=1, replica_groups={{10,0,1,2,3,4,5,6,7,8,9,11,12,13,14,15},{26,16,17,18,19,20,21,22,23,24,..., dimensions={0} | all-to-all | bytes 1048576 | tf_op jit(solution)/shard_map/all_to_all | solution.py:282
  15.9 0.1 shard_map.59
  16.0 12.2 %all_to_all.31 = f32[16,64,128]{2,1,0:T(8,128)S(1)} all-to-all(f32[16,64,128]{2,1,0:T(8,128)S(1)} %shard_map.59), channel_id=1, replica_groups={{10,0,1,2,3,4,5,6,7,8,9,11,12,13,14,15},{26,16,17,18,19,20,21,22,23,24,..., dimensions={0} | all-to-all | bytes 1048576 | tf_op jit(solution)/shard_map/all_to_all | solution.py:286
  28.2 0.9 shard_map.61
  29.0 8.6 %collective-permute-start = (f32[384,128]{1,0:T(8,128)S(1)}, f32[384,128]{1,0:T(8,128)S(1)}, u32[]{:S(2)}, u32[]{:S(2)}) collective-permute-start(f32[384,128]{1,0:T(8,128)S(1)} %shard_map.61), channel_id=1, source_target_pairs={{0,16},{16,0},{32,48},{48,32},{64,80},{80,64},{96,112},{112,96},{1... | collective-permute-start | bytes 589832 | tf_op jit(solution)/shard_map/ppermute | solution.py:300
  37.7 0.9 shard_map.60.x_ref
  38.5 0.2 collective-permute-done.y_ref
  38.7 7.5 %all_to_all.32.x_ref = f32[4,96,128]{2,1,0:T(8,128)S(1)} all-to-all(f32[4,96,128]{2,1,0:T(8,128)S(1)} %bitcast.12), channel_id=1, replica_groups={{64,32,96,0},{80,48,112,16},{192,160,224,128},{208,176,240,144},{320,28..., dimensions={0} | all-to-all | bytes 393216 | tf_op jit(solution)/shard_map/all_to_all | solution.py:304
  46.3 21.9 %all_to_all.33.x_ref = f32[4,96,128]{2,1,0:T(8,128)S(1)} all-to-all(f32[4,96,128]{2,1,0:T(8,128)S(1)} %shard_map.63), channel_id=1, replica_groups={{256,0,128,384},{272,16,144,400},{288,32,160,416},{304,48,176,432},{320..., dimensions={0} | all-to-all | bytes 393216 | tf_op jit(solution)/shard_map/all_to_all | solution.py:308
  68.2 8.6 %all_to_all.34 = f32[4,96,128]{2,1,0:T(8,128)S(1)} all-to-all(f32[4,96,128]{2,1,0:T(8,128)S(1)} %shard_map.64), channel_id=1, replica_groups={{64,32,96,0},{80,48,112,16},{192,160,224,128},{208,176,240,144},{320,28..., dimensions={0} | all-to-all | bytes 393216 | tf_op jit(solution)/shard_map/all_to_all | solution.py:310
  76.7 4.0 %shard_map.65 = (f32[448,128]{1,0:T(8,128)S(1)}, f32[32,8,128]{2,1,0:T(8,128)}) custom-call(f32[384,128]{1,0:T(8,128)S(1)} %bitcast.11), custom_call_target="tpu_custom_call" | custom-call | tf_op jit(solution)/shard_map/pallas_call | solution.py:247
  80.7 5.1 %collective-permute-start.1 = (f32[448,128]{1,0:T(8,128)S(1)}, f32[448,128]{1,0:T(8,128)S(1)}, u32[]{:S(2)}, u32[]{:S(2)}) collective-permute-start(f32[448,128]{1,0:T(8,128)S(1)} %get-tuple-element.16.mine_ref), channel_id=1, source_target_pairs={{0,16},{16,0},{32,48},{48,32},{64,80},{80,64},{96,112},{112,96},{1... | collective-permute-start | bytes 688136 | tf_op jit(solution)/shard_map/ppermute | solution.py:318
  85.9 8.5 %all-to-all-start.5 = ((f32[32,8,128]{2,1,0:T(8,128)}), f32[32,8,128]{2,1,0:T(8,128)S(1)}, u32[]{:S(2)}, u32[]{:S(2)}) async-start(f32[32,8,128]{2,1,0:T(8,128)} %get-tuple-element.15), calls=%async_computation.5 | async-start | bytes 262144 | tf_op jit(solution)/shard_map/all_to_all | solution.py:319
  94.4 0.0 collective-permute-done.1.theirs_ref
  94.4 2.4 %shard_map.66 = (f32[9,224,128]{2,1,0:T(8,128)}, bf16[9,224,256]{2,1,0:T(8,128)(2,1)S(1)}) custom-call(s32[1]{0:T(128)} %bitcast.h_ref.core_ref, f32[448,128]{1,0:T(8,128)S(1)} %get-tuple-element.16.mine_ref, f32[448,128]{1,0:T(8,128)S(1)} %collective-permute-done.1.theirs_ref, f32[9,224,128]{2,1,0:T(8,128)S(1)} %convert_add_fusion.b_ref, ...), custom_call_target="tpu_custom_call" | custom-call | flops 500000000 | bytes 2000000 | tf_op jit(solution)/shard_map/pallas_call | solution.py:247
  96.7 0.5 all-to-all-done.5.n_ref
  97.2 1.4 %shard_map.67 = (bf16[9,224,128]{2,1,0:T(8,128)(2,1)}, f32[9,64,128]{2,1,0:T(8,128)}) custom-call(s32[1]{0:T(128)} %bitcast.h_ref.core_ref, f32[32,8,128]{2,1,0:T(8,128)S(1)} %all-to-all-done.5.n_ref, f32[448,128]{1,0:T(8,128)S(1)} %get-tuple-element.16.mine_ref, f32[448,128]{1,0:T(8,128)S(1)} %collective-permute-done.1.theirs_ref, ...), custom_call_target="tpu_custom_call" | custom-call | tf_op jit(solution)/shard_map/pallas_call | solution.py:247
  (3 shorter events, 0.1 us)
Async XLA Ops:
  0.6 1.5 %copy-start = (f32[9,128,64]{1,2,0:T(8,128)S(1)}, f32[9,128,64]{1,2,0:T(8,128)}, u32[]{:S(2)}) copy-start(f32[9,128,64]{1,2,0:T(8,128)} %param.5) | copy-start | bytes 884740
  29.0 9.7 %collective-permute-start = (f32[384,128]{1,0:T(8,128)S(1)}, f32[384,128]{1,0:T(8,128)S(1)}, u32[]{:S(2)}, u32[]{:S(2)}) collective-permute-start(f32[384,128]{1,0:T(8,128)S(1)} %shard_map.61), channel_id=1, source_target_pairs={{0,16},{16,0},{32,48},{48,32},{64,80},{80,64},{96,112},{112,96},{1... | collective-permute-start | bytes 589832 | tf_op jit(solution)/shard_map/ppermute | solution.py:300
  80.7 13.6 %collective-permute-start.1 = (f32[448,128]{1,0:T(8,128)S(1)}, f32[448,128]{1,0:T(8,128)S(1)}, u32[]{:S(2)}, u32[]{:S(2)}) collective-permute-start(f32[448,128]{1,0:T(8,128)S(1)} %get-tuple-element.16.mine_ref), channel_id=1, source_target_pairs={{0,16},{16,0},{32,48},{48,32},{64,80},{80,64},{96,112},{112,96},{1... | collective-permute-start | bytes 688136 | tf_op jit(solution)/shard_map/ppermute | solution.py:318
  85.9 11.3 %all-to-all-start.5 = ((f32[32,8,128]{2,1,0:T(8,128)}), f32[32,8,128]{2,1,0:T(8,128)S(1)}, u32[]{:S(2)}, u32[]{:S(2)}) async-start(f32[32,8,128]{2,1,0:T(8,128)} %get-tuple-element.15), calls=%async_computation.5 | async-start | bytes 262144 | tf_op jit(solution)/shard_map/all_to_all | solution.py:319

commit v7 on v6

--- a/solution.py
+++ b/solution.py
@@ -43,6 +43,8 @@
     for i in range(mats):
         p = dot(b_ref[i], v_ref[i], 1, 1, 3)
         p_ref[pl.ds(i * half, half), :] = jnp.concatenate([p[:half], p[half:]], axis=1)
+    rest = p_ref.shape[0] - mats * half
+    p_ref[pl.ds(mats * half, rest), :] = jnp.zeros((rest, 128), F32)
 
 
 def sum_kernel(x_ref, o_ref):
@@ -313,7 +315,7 @@
         factor_kernel,
         (shape(FACTOR_ROWS, 128), shape(2 * n_col, 8, 128)),
         reduced.reshape(HALF_ROWS, 128),
-        scratch=(pltpu.VMEM(((FOUR + 1) * rank, 128), F32),) * 2,
+        scratch=(pltpu.VMEM((8 * rank, 128), F32),) * 2,
     )
     theirs = lax.ppermute(mine, "row", swap)
     squares = lax.all_to_all(squares, ("row", "col"), 0, 0, axis_index_groups=plane)

time: 99 us -> 99 us (level)
  no operation moved by 1% of the time
where the time goes in v7:
time: 99 us; the launch traced here: 98.6 us
  blocking collectives  63.3 us (64%)
  starting transfers between devices  22.2 us (22%)
  Pallas kernels  10.3 us (10%)
  other arithmetic  1.48 us (1%)
    all_to_all x1, blocking collectives, on_device(): pieces = lax.all_to_all(summed, 'row', 0, 0, axis_index_groups=far)  21.9 us
    all_to_all x1, blocking collectives, on_device(): lax.all_to_all(part.reshape(n_col, 64, 128), 'col', 0, 0, axis_index_grou...  13.2 us
    all_to_all x1, blocking collectives, on_device(): projected = lax.all_to_all(summed, 'col', 0, 0, axis_index_groups=[order])  12.2 us
    pallas_call x10, Pallas kernels, call(): pl.pallas_call(kernel, out_shape=out, in_specs=(first,) + (vmem,) * (len(...  10.3 us
    ppermute x1, starting transfers between devices, on_device(): theirs = lax.ppermute(products(there), 'row', swap)  8.6 us
    all_to_all x1, blocking collectives, on_device(): reduced = lax.all_to_all(summed, 'row', 0, 0, axis_index_groups=near)  8.56 us
    all_to_all x1, starting transfers between devices, on_device(): lax.all_to_all(squares, ('row', 'col'), 0, 0, axis_index_groups=plane)  8.46 us
    all_to_all x1, blocking collectives, on_device(): lax.all_to_all(pieces.reshape(4, quarter, 128), 'row', 0, 0, axis_index_g...  7.5 us
  transfers between devices with their start and end apart: 3, of which 2 were waited for; matrix products, arithmetic and copies ran while one was open for 0% of the time, Pallas kernels for 3%

profile of v7, /device:TPU:1, one launch (start us, length us, event | category | flops | bytes accessed | tf_op | source)
XLA Modules:
  0.0 98.6 jit_solution(8680146889284608526)
XLA Ops:
  0.6 0.0 copy-start
  0.6 1.5 %convert_add_fusion.b_ref = f32[9,224,128]{2,1,0:T(8,128)S(1)} fusion(f32[9,224,128]{2,1,0:T(8,128)} %param.4, bf16[9,224,128]{2,1,0:T(8,128)(2,1)} %param.3), kind=kLoop, calls=%fused_computation | loop fusion | flops 516096 | bytes 2580480 | tf_op jit(solution)/shard_map/add | solution.py:279
  2.1 0.0 copy-done
  2.1 0.6 shard_map.58
  2.8 13.2 %all_to_all.30.x_ref = f32[16,64,128]{2,1,0:T(8,128)S(1)} all-to-all(f32[16,64,128]{2,1,0:T(8,128)S(1)} %bitcast.10), channel_id=1, replica_groups={{10,0,1,2,3,4,5,6,7,8,9,11,12,13,14,15},{26,16,17,18,19,20,21,22,23,24,..., dimensions={0} | all-to-all | bytes 1048576 | tf_op jit(solution)/shard_map/all_to_all | solution.py:284
  15.9 0.1 shard_map.59
  16.0 12.2 %all_to_all.31 = f32[16,64,128]{2,1,0:T(8,128)S(1)} all-to-all(f32[16,64,128]{2,1,0:T(8,128)S(1)} %shard_map.59), channel_id=1, replica_groups={{10,0,1,2,3,4,5,6,7,8,9,11,12,13,14,15},{26,16,17,18,19,20,21,22,23,24,..., dimensions={0} | all-to-all | bytes 1048576 | tf_op jit(solution)/shard_map/all_to_all | solution.py:288
  28.2 0.9 shard_map.61
  29.0 8.6 %collective-permute-start = (f32[384,128]{1,0:T(8,128)S(1)}, f32[384,128]{1,0:T(8,128)S(1)}, u32[]{:S(2)}, u32[]{:S(2)}) collective-permute-start(f32[384,128]{1,0:T(8,128)S(1)} %shard_map.61), channel_id=1, source_target_pairs={{0,16},{16,0},{32,48},{48,32},{64,80},{80,64},{96,112},{112,96},{1... | collective-permute-start | bytes 589832 | tf_op jit(solution)/shard_map/ppermute | solution.py:302
  37.7 0.9 shard_map.60.x_ref
  38.5 0.2 collective-permute-done.y_ref
  38.7 7.5 %all_to_all.32.x_ref = f32[4,96,128]{2,1,0:T(8,128)S(1)} all-to-all(f32[4,96,128]{2,1,0:T(8,128)S(1)} %bitcast.12), channel_id=1, replica_groups={{64,32,96,0},{80,48,112,16},{192,160,224,128},{208,176,240,144},{320,28..., dimensions={0} | all-to-all | bytes 393216 | tf_op jit(solution)/shard_map/all_to_all | solution.py:306
  46.3 21.9 %all_to_all.33.x_ref = f32[4,96,128]{2,1,0:T(8,128)S(1)} all-to-all(f32[4,96,128]{2,1,0:T(8,128)S(1)} %shard_map.63), channel_id=1, replica_groups={{256,0,128,384},{272,16,144,400},{288,32,160,416},{304,48,176,432},{320..., dimensions={0} | all-to-all | bytes 393216 | tf_op jit(solution)/shard_map/all_to_all | solution.py:310
  68.2 8.6 %all_to_all.34 = f32[4,96,128]{2,1,0:T(8,128)S(1)} all-to-all(f32[4,96,128]{2,1,0:T(8,128)S(1)} %shard_map.64), channel_id=1, replica_groups={{64,32,96,0},{80,48,112,16},{192,160,224,128},{208,176,240,144},{320,28..., dimensions={0} | all-to-all | bytes 393216 | tf_op jit(solution)/shard_map/all_to_all | solution.py:312
  76.7 4.0 %shard_map.65 = (f32[448,128]{1,0:T(8,128)S(1)}, f32[32,8,128]{2,1,0:T(8,128)}) custom-call(f32[384,128]{1,0:T(8,128)S(1)} %bitcast.11), custom_call_target="tpu_custom_call" | custom-call | tf_op jit(solution)/shard_map/pallas_call | solution.py:249
  80.7 5.1 %collective-permute-start.1 = (f32[448,128]{1,0:T(8,128)S(1)}, f32[448,128]{1,0:T(8,128)S(1)}, u32[]{:S(2)}, u32[]{:S(2)}) collective-permute-start(f32[448,128]{1,0:T(8,128)S(1)} %get-tuple-element.16.mine_ref), channel_id=1, source_target_pairs={{0,16},{16,0},{32,48},{48,32},{64,80},{80,64},{96,112},{112,96},{1... | collective-permute-start | bytes 688136 | tf_op jit(solution)/shard_map/ppermute | solution.py:320
  85.9 8.5 %all-to-all-start.5 = ((f32[32,8,128]{2,1,0:T(8,128)}), f32[32,8,128]{2,1,0:T(8,128)S(1)}, u32[]{:S(2)}, u32[]{:S(2)}) async-start(f32[32,8,128]{2,1,0:T(8,128)} %get-tuple-element.15), calls=%async_computation.5 | async-start | bytes 262144 | tf_op jit(solution)/shard_map/all_to_all | solution.py:321
  94.4 0.0 collective-permute-done.1.theirs_ref
  94.4 2.4 %shard_map.66 = (f32[9,224,128]{2,1,0:T(8,128)}, bf16[9,224,256]{2,1,0:T(8,128)(2,1)S(1)}) custom-call(s32[1]{0:T(128)} %bitcast.h_ref.core_ref, f32[448,128]{1,0:T(8,128)S(1)} %get-tuple-element.16.mine_ref, f32[448,128]{1,0:T(8,128)S(1)} %collective-permute-done.1.theirs_ref, f32[9,224,128]{2,1,0:T(8,128)S(1)} %convert_add_fusion.b_ref, ...), custom_call_target="tpu_custom_call" | custom-call | flops 500000000 | bytes 2000000 | tf_op jit(solution)/shard_map/pallas_call | solution.py:249
  96.7 0.5 all-to-all-done.5.n_ref
  97.2 1.4 %shard_map.67 = (bf16[9,224,128]{2,1,0:T(8,128)(2,1)}, f32[9,64,128]{2,1,0:T(8,128)}) custom-call(s32[1]{0:T(128)} %bitcast.h_ref.core_ref, f32[32,8,128]{2,1,0:T(8,128)S(1)} %all-to-all-done.5.n_ref, f32[448,128]{1,0:T(8,128)S(1)} %get-tuple-element.16.mine_ref, f32[448,128]{1,0:T(8,128)S(1)} %collective-permute-done.1.theirs_ref, ...), custom_call_target="tpu_custom_call" | custom-call | tf_op jit(solution)/shard_map/pallas_call | solution.py:249
  (3 shorter events, 0.1 us)
Async XLA Ops:
  0.6 1.5 %copy-start = (f32[9,128,64]{1,2,0:T(8,128)S(1)}, f32[9,128,64]{1,2,0:T(8,128)}, u32[]{:S(2)}) copy-start(f32[9,128,64]{1,2,0:T(8,128)} %param.5) | copy-start | bytes 884740
  29.0 9.7 %collective-permute-start = (f32[384,128]{1,0:T(8,128)S(1)}, f32[384,128]{1,0:T(8,128)S(1)}, u32[]{:S(2)}, u32[]{:S(2)}) collective-permute-start(f32[384,128]{1,0:T(8,128)S(1)} %shard_map.61), channel_id=1, source_target_pairs={{0,16},{16,0},{32,48},{48,32},{64,80},{80,64},{96,112},{112,96},{1... | collective-permute-start | bytes 589832 | tf_op jit(solution)/shard_map/ppermute | solution.py:302
  80.7 13.6 %collective-permute-start.1 = (f32[448,128]{1,0:T(8,128)S(1)}, f32[448,128]{1,0:T(8,128)S(1)}, u32[]{:S(2)}, u32[]{:S(2)}) collective-permute-start(f32[448,128]{1,0:T(8,128)S(1)} %get-tuple-element.16.mine_ref), channel_id=1, source_target_pairs={{0,16},{16,0},{32,48},{48,32},{64,80},{80,64},{96,112},{112,96},{1... | collective-permute-start | bytes 688136 | tf_op jit(solution)/shard_map/ppermute | solution.py:320
  85.9 11.3 %all-to-all-start.5 = ((f32[32,8,128]{2,1,0:T(8,128)}), f32[32,8,128]{2,1,0:T(8,128)S(1)}, u32[]{:S(2)}, u32[]{:S(2)}) async-start(f32[32,8,128]{2,1,0:T(8,128)} %get-tuple-element.15), calls=%async_computation.5 | async-start | bytes 262144 | tf_op jit(solution)/shard_map/all_to_all | solution.py:321

commit v8 on v7

--- a/solution.py
+++ b/solution.py
@@ -179,7 +179,13 @@
         else:
             xt = dot(inv, gy_ref[pl.ds(s * rank, rank), :])
             o_ref[pl.ds(s * rank, rank), :] = xt
-        squares = dot(jnp.ones((8, xt.shape[1]), F32), xt * xt, 1, 1)
+        pieces = jnp.concatenate(parts(xt * xt, 3), axis=1)
+        squares = lax.dot_general(
+            jnp.ones((8, pieces.shape[1]), BF16),
+            pieces,
+            (((1,), (1,)), ((), ())),
+            preferred_element_type=F32,
+        )
         table = jnp.where(row8 == s, jnp.concatenate([squares, zero], axis=1), table)
         o_ref[pl.ds(INVERSES + s * (rank // 2), rank // 2), :] = fold(inv)
     for c in range(n_ref.shape[0]):

time: 99 us -> 98.7 us (level)
  no operation moved by 1% of the time
where the time goes in v8:
time: 98.7 us; the launch traced here: 98.3 us
  blocking collectives  63.3 us (64%)
  starting transfers between devices  22.2 us (22%)
  Pallas kernels  9.97 us (10%)
  other arithmetic  1.48 us (1%)
    all_to_all x1, blocking collectives, on_device(): pieces = lax.all_to_all(summed, 'row', 0, 0, axis_index_groups=far)  21.9 us
    all_to_all x1, blocking collectives, on_device(): lax.all_to_all(part.reshape(n_col, 64, 128), 'col', 0, 0, axis_index_grou...  13.2 us
    all_to_all x1, blocking collectives, on_device(): projected = lax.all_to_all(summed, 'col', 0, 0, axis_index_groups=[order])  12.2 us
    pallas_call x10, Pallas kernels, call(): pl.pallas_call(kernel, out_shape=out, in_specs=(first,) + (vmem,) * (len(...  9.97 us
    ppermute x1, starting transfers between devices, on_device(): theirs = lax.ppermute(products(there), 'row', swap)  8.6 us
    all_to_all x1, blocking collectives, on_device(): reduced = lax.all_to_all(summed, 'row', 0, 0, axis_index_groups=near)  8.56 us
    all_to_all x1, starting transfers between devices, on_device(): lax.all_to_all(squares, ('row', 'col'), 0, 0, axis_index_groups=plane)  8.46 us
    all_to_all x1, blocking collectives, on_device(): lax.all_to_all(pieces.reshape(4, quarter, 128), 'row', 0, 0, axis_index_g...  7.5 us
  transfers between devices with their start and end apart: 3, of which 2 were waited for; matrix products, arithmetic and copies ran while one was open for 0% of the time, Pallas kernels for 3%

profile of v8, /device:TPU:1, one launch (start us, length us, event | category | flops | bytes accessed | tf_op | source)
XLA Modules:
  0.0 98.3 jit_solution(5430941839358950383)
XLA Ops:
  0.6 0.0 copy-start
  0.6 1.5 %convert_add_fusion.b_ref = f32[9,224,128]{2,1,0:T(8,128)S(1)} fusion(f32[9,224,128]{2,1,0:T(8,128)} %param.4, bf16[9,224,128]{2,1,0:T(8,128)(2,1)} %param.3), kind=kLoop, calls=%fused_computation | loop fusion | flops 516096 | bytes 2580480 | tf_op jit(solution)/shard_map/add | solution.py:285
  2.1 0.0 copy-done
  2.1 0.6 shard_map.58
  2.8 13.2 %all_to_all.30.x_ref = f32[16,64,128]{2,1,0:T(8,128)S(1)} all-to-all(f32[16,64,128]{2,1,0:T(8,128)S(1)} %bitcast.10), channel_id=1, replica_groups={{10,0,1,2,3,4,5,6,7,8,9,11,12,13,14,15},{26,16,17,18,19,20,21,22,23,24,..., dimensions={0} | all-to-all | bytes 1048576 | tf_op jit(solution)/shard_map/all_to_all | solution.py:290
  15.9 0.1 shard_map.59
  16.0 12.2 %all_to_all.31 = f32[16,64,128]{2,1,0:T(8,128)S(1)} all-to-all(f32[16,64,128]{2,1,0:T(8,128)S(1)} %shard_map.59), channel_id=1, replica_groups={{10,0,1,2,3,4,5,6,7,8,9,11,12,13,14,15},{26,16,17,18,19,20,21,22,23,24,..., dimensions={0} | all-to-all | bytes 1048576 | tf_op jit(solution)/shard_map/all_to_all | solution.py:294
  28.2 0.9 shard_map.61
  29.0 8.6 %collective-permute-start = (f32[384,128]{1,0:T(8,128)S(1)}, f32[384,128]{1,0:T(8,128)S(1)}, u32[]{:S(2)}, u32[]{:S(2)}) collective-permute-start(f32[384,128]{1,0:T(8,128)S(1)} %shard_map.61), channel_id=1, source_target_pairs={{0,16},{16,0},{32,48},{48,32},{64,80},{80,64},{96,112},{112,96},{1... | collective-permute-start | bytes 589832 | tf_op jit(solution)/shard_map/ppermute | solution.py:308
  37.7 0.9 shard_map.60.x_ref
  38.5 0.2 collective-permute-done.y_ref
  38.7 7.5 %all_to_all.32.x_ref = f32[4,96,128]{2,1,0:T(8,128)S(1)} all-to-all(f32[4,96,128]{2,1,0:T(8,128)S(1)} %bitcast.12), channel_id=1, replica_groups={{64,32,96,0},{80,48,112,16},{192,160,224,128},{208,176,240,144},{320,28..., dimensions={0} | all-to-all | bytes 393216 | tf_op jit(solution)/shard_map/all_to_all | solution.py:312
  46.3 21.9 %all_to_all.33.x_ref = f32[4,96,128]{2,1,0:T(8,128)S(1)} all-to-all(f32[4,96,128]{2,1,0:T(8,128)S(1)} %shard_map.63), channel_id=1, replica_groups={{256,0,128,384},{272,16,144,400},{288,32,160,416},{304,48,176,432},{320..., dimensions={0} | all-to-all | bytes 393216 | tf_op jit(solution)/shard_map/all_to_all | solution.py:316
  68.2 8.6 %all_to_all.34 = f32[4,96,128]{2,1,0:T(8,128)S(1)} all-to-all(f32[4,96,128]{2,1,0:T(8,128)S(1)} %shard_map.64), channel_id=1, replica_groups={{64,32,96,0},{80,48,112,16},{192,160,224,128},{208,176,240,144},{320,28..., dimensions={0} | all-to-all | bytes 393216 | tf_op jit(solution)/shard_map/all_to_all | solution.py:318
  76.7 3.7 %shard_map.65 = (f32[448,128]{1,0:T(8,128)S(1)}, f32[32,8,128]{2,1,0:T(8,128)}) custom-call(f32[384,128]{1,0:T(8,128)S(1)} %bitcast.11), custom_call_target="tpu_custom_call" | custom-call | tf_op jit(solution)/shard_map/pallas_call | solution.py:255
  80.5 5.1 %collective-permute-start.1 = (f32[448,128]{1,0:T(8,128)S(1)}, f32[448,128]{1,0:T(8,128)S(1)}, u32[]{:S(2)}, u32[]{:S(2)}) collective-permute-start(f32[448,128]{1,0:T(8,128)S(1)} %get-tuple-element.16.mine_ref), channel_id=1, source_target_pairs={{0,16},{16,0},{32,48},{48,32},{64,80},{80,64},{96,112},{112,96},{1... | collective-permute-start | bytes 688136 | tf_op jit(solution)/shard_map/ppermute | solution.py:326
  85.6 8.5 %all-to-all-start.5 = ((f32[32,8,128]{2,1,0:T(8,128)}), f32[32,8,128]{2,1,0:T(8,128)S(1)}, u32[]{:S(2)}, u32[]{:S(2)}) async-start(f32[32,8,128]{2,1,0:T(8,128)} %get-tuple-element.15), calls=%async_computation.5 | async-start | bytes 262144 | tf_op jit(solution)/shard_map/all_to_all | solution.py:327
  94.1 0.0 collective-permute-done.1.theirs_ref
  94.1 2.4 %shard_map.66 = (f32[9,224,128]{2,1,0:T(8,128)}, bf16[9,224,256]{2,1,0:T(8,128)(2,1)S(1)}) custom-call(s32[1]{0:T(128)} %bitcast.h_ref.core_ref, f32[448,128]{1,0:T(8,128)S(1)} %get-tuple-element.16.mine_ref, f32[448,128]{1,0:T(8,128)S(1)} %collective-permute-done.1.theirs_ref, f32[9,224,128]{2,1,0:T(8,128)S(1)} %convert_add_fusion.b_ref, ...), custom_call_target="tpu_custom_call" | custom-call | flops 500000000 | bytes 2000000 | tf_op jit(solution)/shard_map/pallas_call | solution.py:255
  96.4 0.5 all-to-all-done.5.n_ref
  96.9 1.4 %shard_map.67 = (bf16[9,224,128]{2,1,0:T(8,128)(2,1)}, f32[9,64,128]{2,1,0:T(8,128)}) custom-call(s32[1]{0:T(128)} %bitcast.h_ref.core_ref, f32[32,8,128]{2,1,0:T(8,128)S(1)} %all-to-all-done.5.n_ref, f32[448,128]{1,0:T(8,128)S(1)} %get-tuple-element.16.mine_ref, f32[448,128]{1,0:T(8,128)S(1)} %collective-permute-done.1.theirs_ref, ...), custom_call_target="tpu_custom_call" | custom-call | tf_op jit(solution)/shard_map/pallas_call | solution.py:255
  (3 shorter events, 0.1 us)
Async XLA Ops:
  0.6 1.5 %copy-start = (f32[9,128,64]{1,2,0:T(8,128)S(1)}, f32[9,128,64]{1,2,0:T(8,128)}, u32[]{:S(2)}) copy-start(f32[9,128,64]{1,2,0:T(8,128)} %param.5) | copy-start | bytes 884740
  29.0 9.7 %collective-permute-start = (f32[384,128]{1,0:T(8,128)S(1)}, f32[384,128]{1,0:T(8,128)S(1)}, u32[]{:S(2)}, u32[]{:S(2)}) collective-permute-start(f32[384,128]{1,0:T(8,128)S(1)} %shard_map.61), channel_id=1, source_target_pairs={{0,16},{16,0},{32,48},{48,32},{64,80},{80,64},{96,112},{112,96},{1... | collective-permute-start | bytes 589832 | tf_op jit(solution)/shard_map/ppermute | solution.py:308
  80.5 13.6 %collective-permute-start.1 = (f32[448,128]{1,0:T(8,128)S(1)}, f32[448,128]{1,0:T(8,128)S(1)}, u32[]{:S(2)}, u32[]{:S(2)}) collective-permute-start(f32[448,128]{1,0:T(8,128)S(1)} %get-tuple-element.16.mine_ref), channel_id=1, source_target_pairs={{0,16},{16,0},{32,48},{48,32},{64,80},{80,64},{96,112},{112,96},{1... | collective-permute-start | bytes 688136 | tf_op jit(solution)/shard_map/ppermute | solution.py:326
  85.6 11.3 %all-to-all-start.5 = ((f32[32,8,128]{2,1,0:T(8,128)}), f32[32,8,128]{2,1,0:T(8,128)S(1)}, u32[]{:S(2)}, u32[]{:S(2)}) async-start(f32[32,8,128]{2,1,0:T(8,128)} %get-tuple-element.15), calls=%async_computation.5 | async-start | bytes 262144 | tf_op jit(solution)/shard_map/all_to_all | solution.py:327
